TPU v7x, 128 devices: a whole 4x4x4 slice. The times are simulated.
128 devices in a mesh: segment: 8 (over z, x_hi), shard: 16 (over y, x_lo, core).
Axes of the slice: x: 4 (x_hi: 2, x_lo: 2; x = x_hi * 2 + x_lo), y: 4, z: 4, core: 2. Of those that a mesh axis runs over, the one named last changes fastest.
Arguments:
- tokens_in: bfloat16 [4, 128, 8192], P(None, 'shard'), may hold values from -20 to 20
- weights: bfloat16 [8, 8192, 8192], P('segment', None, 'shard'), may hold values from -0.0625 to 0.0625
Outputs:
- activations: bfloat16 [8, 4, 128, 8192], P('segment', None, 'shard')
- gram: float32 [8, 8192, 8192], P('segment', 'shard')
All inputs are finite; a program needn't handle non-finite values.
Results may differ from a plain program's by a relative error of at most 0.015.
Values may be sent and summed in bfloat16 or wider, within the bound.
No kernel may reach another device: no remote copies, remote signals or barrier semaphores. Data moves between devices by JAX's collectives and lax.ppermute only.
A program may use at most 192 MiB of HBM per device.

v0:
```python
import jax
import jax.numpy as jnp
from jax import lax
from jax.sharding import PartitionSpec as P

epsilon = 1e-05


def from_behind(block, axis, distance):
    devices = range(lax.axis_size(axis))
    route = [(i - distance, i) for i in devices if i - distance in devices]
    return lax.ppermute(block, axis, route)


def passed_along(value, axis, by):
    devices = lax.axis_size(axis)
    return lax.ppermute(value, axis, [(i, (i + by) % devices) for i in range(devices)])


def gram_piece(gathered, device, block_width, half_count):
    own_columns = lax.dynamic_slice_in_dim(gathered, device * block_width, block_width, 1)
    extended = jnp.concatenate([gathered, gathered[:, : half_count * block_width]], axis=1)
    partner_columns = lax.dynamic_slice_in_dim(
        extended, device * block_width, (half_count + 1) * block_width, 1
    )
    return lax.dot_general(
        own_columns, partner_columns, (((0,), (0,)), ((), ())), preferred_element_type=jnp.float32
    )


def body(tokens_in, weights):
    micro_count, row_count, feature_count = tokens_in.shape
    shard_count = lax.axis_size("shard")
    segment_count = lax.axis_size("segment")
    device = lax.axis_index("shard")
    segment_index = lax.axis_index("segment")
    block_width = feature_count // shard_count
    half_count = shard_count // 2
    batch_rows = row_count * shard_count
    weight_block = weights[0]

    def project(active, gathered):

        def run_product(operand):
            return jnp.dot(operand, weight_block, preferred_element_type=jnp.float32)

        def skip_product(operand):
            return jnp.zeros((operand.shape[0], block_width), jnp.float32)

        return lax.cond(active, run_product, skip_product, gathered)

    def section(current, active):
        floats = current.astype(jnp.float32)
        mean_square = jnp.mean(floats * floats, axis=1, keepdims=True)
        normed = (floats * lax.rsqrt(mean_square + epsilon)).astype(jnp.bfloat16)
        gathered = lax.all_gather(normed, "shard", axis=0, tiled=True)
        product = project(active, gathered)
        returned = lax.all_to_all(product, "shard", split_axis=0, concat_axis=1, tiled=True)
        return ((floats + returned).astype(jnp.bfloat16), gathered)

    state_shape = (row_count, feature_count)
    outputs = jnp.zeros((micro_count,) + state_shape, jnp.bfloat16)
    gram_state = jnp.zeros((block_width, (half_count + 1) * block_width), jnp.float32)

    def tick(tick_index, carry_in):
        carried, outputs, gram_state = carry_in
        micro_index = tick_index - segment_index
        active = (micro_index >= 0) & (micro_index < micro_count)
        clipped = jnp.clip(micro_index, 0, micro_count - 1)
        first_input = lax.dynamic_index_in_dim(tokens_in, clipped, 0, keepdims=False)
        current = jnp.where(segment_index == 0, first_input, carried)
        updated, gathered = section(current, active)
        updated = jnp.where(active, updated, jnp.zeros_like(updated))
        kept = lax.dynamic_index_in_dim(outputs, clipped, 0, keepdims=False)
        outputs = lax.dynamic_update_index_in_dim(
            outputs, jnp.where(active, updated, kept), clipped, 0
        )

        def add_gram(operands):
            state, rows = operands
            return state + gram_piece(rows, device, block_width, half_count)

        def keep_gram(operands):
            return operands[0]

        gram_state = lax.cond(active, add_gram, keep_gram, (gram_state, gathered))
        carried = from_behind(updated, "segment", 1)
        return (carried, outputs, gram_state)

    initial = (jnp.zeros(state_shape, jnp.bfloat16), outputs, gram_state)
    carried, outputs, gram_state = lax.fori_loop(0, micro_count + segment_count - 1, tick, initial)
    gram_sum = gram_state
    gram_sum = gram_sum / (micro_count * batch_rows)
    gram_blocks = [gram_sum]
    for distance in range(half_count - 1, 0, -1):
        tile_block = gram_sum[:, distance * block_width : (distance + 1) * block_width]
        returned_tile = passed_along(tile_block.astype(jnp.bfloat16), "shard", distance).astype(
            tile_block.dtype
        )
        gram_blocks.append(returned_tile.T)
    cyclic_rows = jnp.concatenate(gram_blocks, axis=1)
    doubled = jnp.concatenate([cyclic_rows, cyclic_rows], axis=1)
    offset = (shard_count - device) % shard_count * block_width
    gram_rows = lax.dynamic_slice_in_dim(doubled, offset, feature_count, 1)
    return (outputs[None], gram_rows[None])


def solution(mesh):
    in_specs = (P(None, "shard", None), P("segment", None, "shard"))
    out_specs = (P("segment", None, "shard", None), P("segment", "shard", None))
    return jax.shard_map(body, mesh=mesh, in_specs=in_specs, out_specs=out_specs, check_vma=False)
```

profile of v0, /device:TPU:1, one launch (start us, length us, event | category | flops | bytes accessed | tf_op | source)
XLA Modules:
  0.0 863.6 jit_solution(2151945533109406240)
XLA Ops:
  12.1 719.4 %while.21 = (s32[]{:T(128)}, bf16[8,8192]{1,0:T(8,128)(2,1)S(1)}, bf16[4,8,8192]{2,1,0:T(8,128)(2,1)S(1)}, f32[512,4608]{1,0:T(8,128)}, s32[]{:T(128)}, /*index=...) while((s32[]{:T(128)}, bf16[8,8192]{1,0:T(8,128)(2,1)S(1)}, ...), condition=%wide.region_6.7_spmd, body=%wide.region_0.6_spmd.sunk | while | flops 1683226624 | bytes 44696128 | solution.py:91
  14.0 38.9 %all-gather.2.cloned.1.call-done = bf16[128,8192]{1,0:T(8,128)(2,1)} async-done(((bf16[8,8192]{1,0:T(8,128)(2,1)}), bf16[128,8192]{1,0:T(8,128)(2,1)}) %all-gather.2.cloned.1.call-update) | async-done | bytes 2097168 | tf_op jit(solution)/shard_map/while/body/eval_jaxpr/all_gather | solution.py:56
  63.0 7.2 all-to-all-done
  71.5 10.6 %conditional.5 = (f32[512,4608]{1,0:T(8,128)}) conditional(s32[]{:T(128)} %convert_element_type.71, f32[512,4608]{1,0:T(8,128)} %get-tuple-element.321, (s32[]{:T(128)}, bf16[128,8192]{1,0:T(8,128)(2,1)}, f32[512,4608]{1,0:T(8,128)}) %tuple.70), branch_computations={%region_4.4_spmd, %region_5.5_spmd} | conditional | flops 608698368 | bytes 24248408 | solution.py:86
  72.8 9.3 %convolution_add_fusion = f32[512,4608]{1,0:T(8,128)} fusion(f32[512,4608]{1,0:T(8,128)} %get-tuple-element.194, s32[]{:T(128)S(6)} %select_n.58, bf16[128,8192]{1,0:T(8,128)(2,1)} %get-tuple-element.195, bf16[128,4096]{1,0:T(8,128)(2,1)S(1)} %slice.23, s32[]{:T(128)S(6)} %select_n.57), kind=kOutput, calls=%fused_computation | convolution fusion | flops 608698368 | bytes 22151176 | tf_op jit(solution)/shard_map/while/body/eval_jaxpr/cond/branch_1_fun/dot_general | solution.py:26
  84.0 30.1 %all-gather.2.cloned.1.call-done = bf16[128,8192]{1,0:T(8,128)(2,1)} async-done(((bf16[8,8192]{1,0:T(8,128)(2,1)}), bf16[128,8192]{1,0:T(8,128)(2,1)}) %all-gather.2.cloned.1.call-update) | async-done | bytes 2097168 | tf_op jit(solution)/shard_map/while/body/eval_jaxpr/all_gather | solution.py:56
  124.2 7.2 all-to-all-done
  135.7 10.6 %conditional.5 = (f32[512,4608]{1,0:T(8,128)}) conditional(s32[]{:T(128)} %convert_element_type.71, f32[512,4608]{1,0:T(8,128)} %get-tuple-element.321, (s32[]{:T(128)}, bf16[128,8192]{1,0:T(8,128)(2,1)}, f32[512,4608]{1,0:T(8,128)}) %tuple.70), branch_computations={%region_4.4_spmd, %region_5.5_spmd} | conditional | flops 608698368 | bytes 24248408 | solution.py:86
  137.0 9.3 %convolution_add_fusion = f32[512,4608]{1,0:T(8,128)} fusion(f32[512,4608]{1,0:T(8,128)} %get-tuple-element.194, s32[]{:T(128)S(6)} %select_n.58, bf16[128,8192]{1,0:T(8,128)(2,1)} %get-tuple-element.195, bf16[128,4096]{1,0:T(8,128)(2,1)S(1)} %slice.23, s32[]{:T(128)S(6)} %select_n.57), kind=kOutput, calls=%fused_computation | convolution fusion | flops 608698368 | bytes 22151176 | tf_op jit(solution)/shard_map/while/body/eval_jaxpr/cond/branch_1_fun/dot_general | solution.py:26
  148.2 30.3 %all-gather.2.cloned.1.call-done = bf16[128,8192]{1,0:T(8,128)(2,1)} async-done(((bf16[8,8192]{1,0:T(8,128)(2,1)}), bf16[128,8192]{1,0:T(8,128)(2,1)}) %all-gather.2.cloned.1.call-update) | async-done | bytes 2097168 | tf_op jit(solution)/shard_map/while/body/eval_jaxpr/all_gather | solution.py:56
  188.6 7.2 all-to-all-done
  200.1 10.6 %conditional.5 = (f32[512,4608]{1,0:T(8,128)}) conditional(s32[]{:T(128)} %convert_element_type.71, f32[512,4608]{1,0:T(8,128)} %get-tuple-element.321, (s32[]{:T(128)}, bf16[128,8192]{1,0:T(8,128)(2,1)}, f32[512,4608]{1,0:T(8,128)}) %tuple.70), branch_computations={%region_4.4_spmd, %region_5.5_spmd} | conditional | flops 608698368 | bytes 24248408 | solution.py:86
  201.4 9.3 %convolution_add_fusion = f32[512,4608]{1,0:T(8,128)} fusion(f32[512,4608]{1,0:T(8,128)} %get-tuple-element.194, s32[]{:T(128)S(6)} %select_n.58, bf16[128,8192]{1,0:T(8,128)(2,1)} %get-tuple-element.195, bf16[128,4096]{1,0:T(8,128)(2,1)S(1)} %slice.23, s32[]{:T(128)S(6)} %select_n.57), kind=kOutput, calls=%fused_computation | convolution fusion | flops 608698368 | bytes 22151176 | tf_op jit(solution)/shard_map/while/body/eval_jaxpr/cond/branch_1_fun/dot_general | solution.py:26
  212.6 31.3 %all-gather.2.cloned.1.call-done = bf16[128,8192]{1,0:T(8,128)(2,1)} async-done(((bf16[8,8192]{1,0:T(8,128)(2,1)}), bf16[128,8192]{1,0:T(8,128)(2,1)}) %all-gather.2.cloned.1.call-update) | async-done | bytes 2097168 | tf_op jit(solution)/shard_map/while/body/eval_jaxpr/all_gather | solution.py:56
  254.0 7.2 all-to-all-done
  265.5 10.6 %conditional.5 = (f32[512,4608]{1,0:T(8,128)}) conditional(s32[]{:T(128)} %convert_element_type.71, f32[512,4608]{1,0:T(8,128)} %get-tuple-element.321, (s32[]{:T(128)}, bf16[128,8192]{1,0:T(8,128)(2,1)}, f32[512,4608]{1,0:T(8,128)}) %tuple.70), branch_computations={%region_4.4_spmd, %region_5.5_spmd} | conditional | flops 608698368 | bytes 24248408 | solution.py:86
  266.8 9.3 %convolution_add_fusion = f32[512,4608]{1,0:T(8,128)} fusion(f32[512,4608]{1,0:T(8,128)} %get-tuple-element.194, s32[]{:T(128)S(6)} %select_n.58, bf16[128,8192]{1,0:T(8,128)(2,1)} %get-tuple-element.195, bf16[128,4096]{1,0:T(8,128)(2,1)S(1)} %slice.23, s32[]{:T(128)S(6)} %select_n.57), kind=kOutput, calls=%fused_computation | convolution fusion | flops 608698368 | bytes 22151176 | tf_op jit(solution)/shard_map/while/body/eval_jaxpr/cond/branch_1_fun/dot_general | solution.py:26
  278.0 31.4 %all-gather.2.cloned.1.call-done = bf16[128,8192]{1,0:T(8,128)(2,1)} async-done(((bf16[8,8192]{1,0:T(8,128)(2,1)}), bf16[128,8192]{1,0:T(8,128)(2,1)}) %all-gather.2.cloned.1.call-update) | async-done | bytes 2097168 | tf_op jit(solution)/shard_map/while/body/eval_jaxpr/all_gather | solution.py:56
  314.2 7.2 all-to-all-done
  321.4 9.5 %collective-permute-start = (bf16[8,8192]{1,0:T(8,128)(2,1)S(1)}, bf16[8,8192]{1,0:T(8,128)(2,1)S(1)}, u32[]{:S(2)}, u32[]{:S(2)}) collective-permute-start(bf16[8,8192]{1,0:T(8,128)(2,1)S(1)} %get-tuple-element.303), channel_id=1, source_target_pairs={{0,16},{16,32},{32,48},{48,64},{64,80},{80,96},{96,112},{1,17},{17... | collective-permute-start | bytes 393224 | tf_op jit(solution)/shard_map/while/body/eval_jaxpr/ppermute | solution.py:12
  334.7 41.0 %all-gather.2.cloned.1.call-done = bf16[128,8192]{1,0:T(8,128)(2,1)} async-done(((bf16[8,8192]{1,0:T(8,128)(2,1)}), bf16[128,8192]{1,0:T(8,128)(2,1)}) %all-gather.2.cloned.1.call-update) | async-done | bytes 2097168 | tf_op jit(solution)/shard_map/while/body/eval_jaxpr/all_gather | solution.py:56
  380.6 7.2 all-to-all-done
  395.9 46.9 %all-gather.2.cloned.1.call-done = bf16[128,8192]{1,0:T(8,128)(2,1)} async-done(((bf16[8,8192]{1,0:T(8,128)(2,1)}), bf16[128,8192]{1,0:T(8,128)(2,1)}) %all-gather.2.cloned.1.call-update) | async-done | bytes 2097168 | tf_op jit(solution)/shard_map/while/body/eval_jaxpr/all_gather | solution.py:56
  462.9 47.9 %all-gather.2.cloned.1.call-done = bf16[128,8192]{1,0:T(8,128)(2,1)} async-done(((bf16[8,8192]{1,0:T(8,128)(2,1)}), bf16[128,8192]{1,0:T(8,128)(2,1)}) %all-gather.2.cloned.1.call-update) | async-done | bytes 2097168 | tf_op jit(solution)/shard_map/while/body/eval_jaxpr/all_gather | solution.py:56
  530.9 47.9 %all-gather.2.cloned.1.call-done = bf16[128,8192]{1,0:T(8,128)(2,1)} async-done(((bf16[8,8192]{1,0:T(8,128)(2,1)}), bf16[128,8192]{1,0:T(8,128)(2,1)}) %all-gather.2.cloned.1.call-update) | async-done | bytes 2097168 | tf_op jit(solution)/shard_map/while/body/eval_jaxpr/all_gather | solution.py:56
  598.9 47.6 %all-gather.2.cloned.1.call-done = bf16[128,8192]{1,0:T(8,128)(2,1)} async-done(((bf16[8,8192]{1,0:T(8,128)(2,1)}), bf16[128,8192]{1,0:T(8,128)(2,1)}) %all-gather.2.cloned.1.call-update) | async-done | bytes 2097168 | tf_op jit(solution)/shard_map/while/body/eval_jaxpr/all_gather | solution.py:56
  666.6 46.7 %all-gather.2.cloned.1.call-done = bf16[128,8192]{1,0:T(8,128)(2,1)} async-done(((bf16[8,8192]{1,0:T(8,128)(2,1)}), bf16[128,8192]{1,0:T(8,128)(2,1)}) %all-gather.2.cloned.1.call-update) | async-done | bytes 2097168 | tf_op jit(solution)/shard_map/while/body/eval_jaxpr/all_gather | solution.py:56
  757.6 8.0 constant_dynamic-update-slice_fusion.1
  765.6 37.8 %collective-permute-done.1 = bf16[512,512]{0,1:T(8,128)(2,1)S(1)} collective-permute-done((bf16[512,512]{0,1:T(8,128)(2,1)}, bf16[512,512]{0,1:T(8,128)(2,1)S(1)}, u32[]{:S(2)}, u32[]{:S(2)}) %collective-permute-start.1) | collective-permute-done | bytes 524320 | tf_op jit(solution)/shard_map/ppermute | solution.py:17
  805.5 18.6 %collective-permute-done.3 = bf16[512,512]{0,1:T(8,128)(2,1)S(1)} collective-permute-done((bf16[512,512]{0,1:T(8,128)(2,1)}, bf16[512,512]{0,1:T(8,128)(2,1)S(1)}, u32[]{:S(2)}, u32[]{:S(2)}) %collective-permute-start.3) | collective-permute-done | bytes 524320 | tf_op jit(solution)/shard_map/ppermute | solution.py:17
  829.7 7.9 constant_dynamic-update-slice_fusion
  845.4 11.7 %dynamic-slice_bitcast_fusion = f32[1,512,8192]{2,1,0:T(8,128)} fusion(f32[512,16384]{1,0:T(8,128)} %bitcast_dynamic-update-slice_fusion.2, s32[]{:T(128)S(6)} %select_n.67), kind=kLoop, calls=%fused_computation.19 | loop fusion | bytes 33554436 | tf_op jit(solution)/shard_map/broadcast_in_dim | solution.py:105
  (181 shorter events, 264.7 us)
Async XLA Ops:
  12.1 40.8 %all-gather.2.cloned.1.call-start = ((), (), s32[]{:S(2)}) async-start(), calls=%async_computation.1 | async-start | bytes 2228224 | tf_op jit(solution)/shard_map/while/body/eval_jaxpr/all_gather | solution.py:56
  70.2 11.9 %collective-permute-start = (bf16[8,8192]{1,0:T(8,128)(2,1)S(1)}, bf16[8,8192]{1,0:T(8,128)(2,1)S(1)}, u32[]{:S(2)}, u32[]{:S(2)}) collective-permute-start(bf16[8,8192]{1,0:T(8,128)(2,1)S(1)} %get-tuple-element.303), channel_id=1, source_target_pairs={{0,16},{16,32},{32,48},{48,64},{64,80},{80,96},{96,112},{1,17},{17... | collective-permute-start | bytes 393224 | tf_op jit(solution)/shard_map/while/body/eval_jaxpr/ppermute | solution.py:12
  82.1 32.0 %all-gather.2.cloned.1.call-start = ((), (), s32[]{:S(2)}) async-start(), calls=%async_computation.1 | async-start | bytes 2228224 | tf_op jit(solution)/shard_map/while/body/eval_jaxpr/all_gather | solution.py:56
  120.1 11.2 %all-to-all-start = ((f32[16,8,512]{2,1,0:T(8,128)}), f32[16,8,512]{2,1,0:T(8,128)S(1)}, u32[]{:S(2)}, u32[]{:S(2)}) async-start(f32[16,8,512]{2,1,0:T(8,128)} %bitcast.46), calls=%async_computation | async-start | bytes 524288 | tf_op jit(solution)/shard_map/while/body/eval_jaxpr/all_to_all | solution.py:58
  131.4 14.9 %collective-permute-start = (bf16[8,8192]{1,0:T(8,128)(2,1)S(1)}, bf16[8,8192]{1,0:T(8,128)(2,1)S(1)}, u32[]{:S(2)}, u32[]{:S(2)}) collective-permute-start(bf16[8,8192]{1,0:T(8,128)(2,1)S(1)} %get-tuple-element.303), channel_id=1, source_target_pairs={{0,16},{16,32},{32,48},{48,64},{64,80},{80,96},{96,112},{1,17},{17... | collective-permute-start | bytes 393224 | tf_op jit(solution)/shard_map/while/body/eval_jaxpr/ppermute | solution.py:12
  146.3 32.2 %all-gather.2.cloned.1.call-start = ((), (), s32[]{:S(2)}) async-start(), calls=%async_computation.1 | async-start | bytes 2228224 | tf_op jit(solution)/shard_map/while/body/eval_jaxpr/all_gather | solution.py:56
  195.8 14.9 %collective-permute-start = (bf16[8,8192]{1,0:T(8,128)(2,1)S(1)}, bf16[8,8192]{1,0:T(8,128)(2,1)S(1)}, u32[]{:S(2)}, u32[]{:S(2)}) collective-permute-start(bf16[8,8192]{1,0:T(8,128)(2,1)S(1)} %get-tuple-element.303), channel_id=1, source_target_pairs={{0,16},{16,32},{32,48},{48,64},{64,80},{80,96},{96,112},{1,17},{17... | collective-permute-start | bytes 393224 | tf_op jit(solution)/shard_map/while/body/eval_jaxpr/ppermute | solution.py:12
  210.7 33.2 %all-gather.2.cloned.1.call-start = ((), (), s32[]{:S(2)}) async-start(), calls=%async_computation.1 | async-start | bytes 2228224 | tf_op jit(solution)/shard_map/while/body/eval_jaxpr/all_gather | solution.py:56
  249.9 11.2 %all-to-all-start = ((f32[16,8,512]{2,1,0:T(8,128)}), f32[16,8,512]{2,1,0:T(8,128)S(1)}, u32[]{:S(2)}, u32[]{:S(2)}) async-start(f32[16,8,512]{2,1,0:T(8,128)} %bitcast.46), calls=%async_computation | async-start | bytes 524288 | tf_op jit(solution)/shard_map/while/body/eval_jaxpr/all_to_all | solution.py:58
  261.2 14.9 %collective-permute-start = (bf16[8,8192]{1,0:T(8,128)(2,1)S(1)}, bf16[8,8192]{1,0:T(8,128)(2,1)S(1)}, u32[]{:S(2)}, u32[]{:S(2)}) collective-permute-start(bf16[8,8192]{1,0:T(8,128)(2,1)S(1)} %get-tuple-element.303), channel_id=1, source_target_pairs={{0,16},{16,32},{32,48},{48,64},{64,80},{80,96},{96,112},{1,17},{17... | collective-permute-start | bytes 393224 | tf_op jit(solution)/shard_map/while/body/eval_jaxpr/ppermute | solution.py:12
  276.1 33.2 %all-gather.2.cloned.1.call-start = ((), (), s32[]{:S(2)}) async-start(), calls=%async_computation.1 | async-start | bytes 2228224 | tf_op jit(solution)/shard_map/while/body/eval_jaxpr/all_gather | solution.py:56
  310.1 11.2 %all-to-all-start = ((f32[16,8,512]{2,1,0:T(8,128)}), f32[16,8,512]{2,1,0:T(8,128)S(1)}, u32[]{:S(2)}, u32[]{:S(2)}) async-start(f32[16,8,512]{2,1,0:T(8,128)} %bitcast.46), calls=%async_computation | async-start | bytes 524288 | tf_op jit(solution)/shard_map/while/body/eval_jaxpr/all_to_all | solution.py:58
  321.4 11.5 %collective-permute-start = (bf16[8,8192]{1,0:T(8,128)(2,1)S(1)}, bf16[8,8192]{1,0:T(8,128)(2,1)S(1)}, u32[]{:S(2)}, u32[]{:S(2)}) collective-permute-start(bf16[8,8192]{1,0:T(8,128)(2,1)S(1)} %get-tuple-element.303), channel_id=1, source_target_pairs={{0,16},{16,32},{32,48},{48,64},{64,80},{80,96},{96,112},{1,17},{17... | collective-permute-start | bytes 393224 | tf_op jit(solution)/shard_map/while/body/eval_jaxpr/ppermute | solution.py:12
  332.8 42.9 %all-gather.2.cloned.1.call-start = ((), (), s32[]{:S(2)}) async-start(), calls=%async_computation.1 | async-start | bytes 2228224 | tf_op jit(solution)/shard_map/while/body/eval_jaxpr/all_gather | solution.py:56
  376.5 11.2 %all-to-all-start = ((f32[16,8,512]{2,1,0:T(8,128)}), f32[16,8,512]{2,1,0:T(8,128)S(1)}, u32[]{:S(2)}, u32[]{:S(2)}) async-start(f32[16,8,512]{2,1,0:T(8,128)} %bitcast.46), calls=%async_computation | async-start | bytes 524288 | tf_op jit(solution)/shard_map/while/body/eval_jaxpr/all_to_all | solution.py:58
  394.0 48.8 %all-gather.2.cloned.1.call-start = ((), (), s32[]{:S(2)}) async-start(), calls=%async_computation.1 | async-start | bytes 2228224 | tf_op jit(solution)/shard_map/while/body/eval_jaxpr/all_gather | solution.py:56
  443.5 11.2 %all-to-all-start = ((f32[16,8,512]{2,1,0:T(8,128)}), f32[16,8,512]{2,1,0:T(8,128)S(1)}, u32[]{:S(2)}, u32[]{:S(2)}) async-start(f32[16,8,512]{2,1,0:T(8,128)} %bitcast.46), calls=%async_computation | async-start | bytes 524288 | tf_op jit(solution)/shard_map/while/body/eval_jaxpr/all_to_all | solution.py:58
  461.0 49.8 %all-gather.2.cloned.1.call-start = ((), (), s32[]{:S(2)}) async-start(), calls=%async_computation.1 | async-start | bytes 2228224 | tf_op jit(solution)/shard_map/while/body/eval_jaxpr/all_gather | solution.py:56
  511.5 11.2 %all-to-all-start = ((f32[16,8,512]{2,1,0:T(8,128)}), f32[16,8,512]{2,1,0:T(8,128)S(1)}, u32[]{:S(2)}, u32[]{:S(2)}) async-start(f32[16,8,512]{2,1,0:T(8,128)} %bitcast.46), calls=%async_computation | async-start | bytes 524288 | tf_op jit(solution)/shard_map/while/body/eval_jaxpr/all_to_all | solution.py:58
  529.0 49.8 %all-gather.2.cloned.1.call-start = ((), (), s32[]{:S(2)}) async-start(), calls=%async_computation.1 | async-start | bytes 2228224 | tf_op jit(solution)/shard_map/while/body/eval_jaxpr/all_gather | solution.py:56
  579.5 11.2 %all-to-all-start = ((f32[16,8,512]{2,1,0:T(8,128)}), f32[16,8,512]{2,1,0:T(8,128)S(1)}, u32[]{:S(2)}, u32[]{:S(2)}) async-start(f32[16,8,512]{2,1,0:T(8,128)} %bitcast.46), calls=%async_computation | async-start | bytes 524288 | tf_op jit(solution)/shard_map/while/body/eval_jaxpr/all_to_all | solution.py:58
  597.0 49.5 %all-gather.2.cloned.1.call-start = ((), (), s32[]{:S(2)}) async-start(), calls=%async_computation.1 | async-start | bytes 2228224 | tf_op jit(solution)/shard_map/while/body/eval_jaxpr/all_gather | solution.py:56
  647.3 11.2 %all-to-all-start = ((f32[16,8,512]{2,1,0:T(8,128)}), f32[16,8,512]{2,1,0:T(8,128)S(1)}, u32[]{:S(2)}, u32[]{:S(2)}) async-start(f32[16,8,512]{2,1,0:T(8,128)} %bitcast.46), calls=%async_computation | async-start | bytes 524288 | tf_op jit(solution)/shard_map/while/body/eval_jaxpr/all_to_all | solution.py:58
  664.8 48.6 %all-gather.2.cloned.1.call-start = ((), (), s32[]{:S(2)}) async-start(), calls=%async_computation.1 | async-start | bytes 2228224 | tf_op jit(solution)/shard_map/while/body/eval_jaxpr/all_gather | solution.py:56
  714.1 11.2 %all-to-all-start = ((f32[16,8,512]{2,1,0:T(8,128)}), f32[16,8,512]{2,1,0:T(8,128)S(1)}, u32[]{:S(2)}, u32[]{:S(2)}) async-start(f32[16,8,512]{2,1,0:T(8,128)} %bitcast.46), calls=%async_computation | async-start | bytes 524288 | tf_op jit(solution)/shard_map/while/body/eval_jaxpr/all_to_all | solution.py:58
  749.1 79.5 %collective-permute-start.7 = (bf16[512,512]{0,1:T(8,128)(2,1)}, bf16[512,512]{0,1:T(8,128)(2,1)S(1)}, u32[]{:S(2)}, u32[]{:S(2)}) collective-permute-start(bf16[512,512]{0,1:T(8,128)(2,1)} %get-tuple-element.235), channel_id=1, source_target_pairs={{0,1},{1,2},{2,3},{3,4},{4,5},{5,6},{6,7},{7,8},{8,9},{9,10},{10,1... | collective-permute-start | bytes 1572872 | tf_op jit(solution)/shard_map/ppermute | solution.py:17
  751.1 76.4 %collective-permute-start.6 = (bf16[512,512]{0,1:T(8,128)(2,1)}, bf16[512,512]{0,1:T(8,128)(2,1)S(1)}, u32[]{:S(2)}, u32[]{:S(2)}) collective-permute-start(bf16[512,512]{0,1:T(8,128)(2,1)} %get-tuple-element.236), channel_id=1, source_target_pairs={{0,2},{1,3},{2,4},{3,5},{4,6},{5,7},{6,8},{7,9},{8,10},{9,11},{10,... | collective-permute-start | bytes 1572872 | tf_op jit(solution)/shard_map/ppermute | solution.py:17
  752.2 74.2 %collective-permute-start.5 = (bf16[512,512]{0,1:T(8,128)(2,1)}, bf16[512,512]{0,1:T(8,128)(2,1)S(1)}, u32[]{:S(2)}, u32[]{:S(2)}) collective-permute-start(bf16[512,512]{0,1:T(8,128)(2,1)} %get-tuple-element.237), channel_id=1, source_target_pairs={{0,3},{1,4},{2,5},{3,6},{4,7},{5,8},{6,9},{7,10},{8,11},{9,12},{10... | collective-permute-start | bytes 1572872 | tf_op jit(solution)/shard_map/ppermute | solution.py:17
  752.2 52.2 %collective-permute-start.2 = (bf16[512,512]{0,1:T(8,128)(2,1)}, bf16[512,512]{0,1:T(8,128)(2,1)S(1)}, u32[]{:S(2)}, u32[]{:S(2)}) collective-permute-start(bf16[512,512]{0,1:T(8,128)(2,1)} %get-tuple-element.240), channel_id=1, source_target_pairs={{0,6},{1,7},{2,8},{3,9},{4,10},{5,11},{6,12},{7,13},{8,14},{9,15},... | collective-permute-start | bytes 1572872 | tf_op jit(solution)/shard_map/ppermute | solution.py:17
  753.7 49.6 %collective-permute-start.1 = (bf16[512,512]{0,1:T(8,128)(2,1)}, bf16[512,512]{0,1:T(8,128)(2,1)S(1)}, u32[]{:S(2)}, u32[]{:S(2)}) collective-permute-start(bf16[512,512]{0,1:T(8,128)(2,1)} %get-tuple-element.241), channel_id=1, source_target_pairs={{0,7},{1,8},{2,9},{3,10},{4,11},{5,12},{6,13},{7,14},{8,15},{9,0},... | collective-permute-start | bytes 1572872 | tf_op jit(solution)/shard_map/ppermute | solution.py:17
  803.3 20.8 %collective-permute-start.3 = (bf16[512,512]{0,1:T(8,128)(2,1)}, bf16[512,512]{0,1:T(8,128)(2,1)S(1)}, u32[]{:S(2)}, u32[]{:S(2)}) collective-permute-start(bf16[512,512]{0,1:T(8,128)(2,1)} %get-tuple-element.239), channel_id=1, source_target_pairs={{0,5},{1,6},{2,7},{3,8},{4,9},{5,10},{6,11},{7,12},{8,13},{9,14},{... | collective-permute-start | bytes 1572872 | tf_op jit(solution)/shard_map/ppermute | solution.py:17
  804.4 20.9 %collective-permute-start.4 = (bf16[512,512]{0,1:T(8,128)(2,1)}, bf16[512,512]{0,1:T(8,128)(2,1)S(1)}, u32[]{:S(2)}, u32[]{:S(2)}) collective-permute-start(bf16[512,512]{0,1:T(8,128)(2,1)} %get-tuple-element.238), channel_id=1, source_target_pairs={{0,4},{1,5},{2,6},{3,7},{4,8},{5,9},{6,10},{7,11},{8,12},{9,13},{1... | collective-permute-start | bytes 1572872 | tf_op jit(solution)/shard_map/ppermute | solution.py:17
  (9 other events, 165.8 us)
Sparse Core Ops, SparseCore 0:
  15.2 37.6 all-gather.1
  85.2 28.8 all-gather.1
  149.4 29.0 all-gather.1
  213.5 30.3 all-gather.1
  278.9 30.4 all-gather.1
  335.6 40.0 all-gather.1
  397.1 45.6 all-gather.1
  464.1 46.6 all-gather.1
  532.1 46.6 all-gather.1
  599.8 46.6 all-gather.1
  667.9 45.4 all-gather.1
where the time goes:
time: 877 us; the launch traced here: 864 us
  waiting for transfers between devices  589 us (67%)
  starting transfers between devices  103 us (12%)
  matrix products  61.1 us (7%)
  other arithmetic  59.2 us (7%)
  local copies, waits for them, and re-layouts  37.6 us (4%)
  between operations  13.7 us (2%)
    all_gather x11, waiting for transfers between devices, section(): gathered = lax.all_gather(normed, 'shard', axis=0, tiled=True)  440 us
    all_to_all x11, waiting for transfers between devices, section(): lax.all_to_all(product, 'shard', split_axis=0, concat_axis=1, tiled=True)  78.7 us
    ppermute x7, waiting for transfers between devices, passed_along(): lax.ppermute(value, axis, [(i, (i + by) % devices) for i in range(devices)])  56.5 us
    ppermute x11, starting transfers between devices, from_behind(): return lax.ppermute(block, axis, route)  49.3 us
    all_to_all x11, starting transfers between devices, section(): lax.all_to_all(product, 'shard', split_axis=0, concat_axis=1, tiled=True)  44.7 us
    dot_general x4, matrix products, gram_piece(): lax.dot_general(own_columns, partner_columns, (((0,), (0,)), ((), ())), p...  37.2 us
    unnamed x15, other arithmetic  30.2 us
    dot_general x4, matrix products, run_product(): return jnp.dot(operand, weight_block, preferred_element_type=jnp.float32)  23.9 us
  transfers between devices with their start and end apart: 40, of which 32 were waited for; matrix products, arithmetic and copies ran while one was open for 7% of the time, Pallas kernels for 0%

commit v1 on v0

v1 whole, which is shorter than its diff:
```python
import jax
import jax.numpy as jnp
from jax import lax
from jax.sharding import PartitionSpec as P

epsilon = 1e-05
AXES = ("segment", "shard")
SEGMENTS, ROWS, COLUMNS, CORES = 8, 4, 2, 2


def shard_of(row, column, core):
    return (row * COLUMNS + column) * CORES + core


def move(value, segments, target):
    pairs = []
    for s in segments:
        for row in range(ROWS):
            for column in range(COLUMNS):
                for core in range(CORES):
                    t, r, c, k = target(s, row, column, core)
                    pairs.append((s * 16 + shard_of(row, column, core), t * 16 + shard_of(r % ROWS, c, k)))
    return lax.ppermute(value, AXES, pairs)


def to_sibling(value, segments):
    return move(value, segments, lambda s, r, c, k: (s, r, c, 1 - k))


def up_rows(value, segments, by):
    return move(value, segments, lambda s, r, c, k: (s, r + by, c, k))


def next_segment(value, segments):
    return move(value, segments, lambda s, r, c, k: (s + 1, r, k, c))


def body(tokens_in, weights):
    micros, rows, features = tokens_in.shape
    shards = 16
    batch = rows * shards
    block = features // 8
    half = block // 2
    device = lax.axis_index("shard")
    segment = lax.axis_index("segment")
    core = device % 2
    column = device // 2 % 2
    row = device // 4
    everyone = range(SEGMENTS)

    pieces = weights[0].reshape(ROWS, COLUMNS, block, half)
    order = [0, 1, 3, 2]

    def rows_of(which):
        parts = [lax.dynamic_slice(pieces, ((row + ROWS - by) % ROWS, which, 0, 0), (1, 1, block, half)) for by in order]
        return jnp.concatenate([p[0, 0] for p in parts], axis=0)

    kept = rows_of(core)
    swapped = to_sibling(rows_of(1 - core), everyone)

    split = tokens_in.reshape(micros, rows, ROWS, COLUMNS, block)
    outgoing = jnp.stack([split[:, :, r, k] for r in range(ROWS) for c in range(COLUMNS) for k in range(CORES)])
    arrived = lax.all_to_all(outgoing, "shard", 0, 0)
    tokens = arrived.transpose(1, 0, 2, 3).reshape(micros, batch, block)

    normed_all = jnp.zeros((micros, batch, features), jnp.bfloat16)
    acts_all = jnp.zeros((micros, batch, half), jnp.bfloat16)
    chip_block = None
    for tick in range(micros + SEGMENTS - 1):
        live = [s for s in everyone if 0 <= tick - s < micros]
        group = tick - segment
        slot = jnp.clip(group, 0, micros - 1)
        if tick == 0:
            held = tokens[0]
        else:
            held = next_segment(chip_block, [s - 1 for s in live if s > 0])
            if tick < micros:
                held = jnp.where(segment == 0, tokens[tick], held)
        gathered = [held] + [up_rows(held, live, by) for by in order[1:]]
        other_held = to_sibling(held, live)
        inputs = jnp.concatenate(gathered, axis=1)
        floats = inputs.astype(jnp.float32)
        squares = jnp.sum(floats * floats, axis=1, keepdims=True)
        mine = jnp.dot(inputs, kept, preferred_element_type=jnp.float32)
        others = jnp.dot(inputs, swapped, preferred_element_type=jnp.float32)
        summary = jnp.broadcast_to(squares, (batch, 128))
        came = to_sibling(jnp.concatenate([mine, others, summary], axis=1), live)
        total = squares + came[:, 2 * half : 2 * half + 1]
        scale = lax.rsqrt(total / features + epsilon)
        mine = mine + came[:, half : 2 * half]
        others = others + came[:, :half]
        product = jnp.where(core == 0, jnp.concatenate([mine, others], 1), jnp.concatenate([others, mine], 1))
        residual = jnp.where(core == column, held, other_held)
        chip_block = (residual.astype(jnp.float32) + product * scale).astype(jnp.bfloat16)
        own = lax.dynamic_slice(chip_block, (0, core * half), (batch, half))
        sibling_rest = to_sibling(inputs[:, block:], live)
        full = jnp.zeros((batch, features), jnp.bfloat16)
        for which, blocks in ((core, gathered), (1 - core, [other_held] + [sibling_rest[:, i * block : (i + 1) * block] for i in range(3)])):
            for by, part in zip(order, blocks):
                place = ((row + ROWS - by) % ROWS * COLUMNS + which) * block
                full = lax.dynamic_update_slice(full, part, (0, place))
        normed = (full.astype(jnp.float32) * scale).astype(jnp.bfloat16)
        if tick >= micros:
            active = group < micros
            normed = jnp.where(active, normed, lax.dynamic_index_in_dim(normed_all, slot, 0, keepdims=False))
            own = jnp.where(active, own, lax.dynamic_index_in_dim(acts_all, slot, 0, keepdims=False))
        normed_all = lax.dynamic_update_index_in_dim(normed_all, normed, slot, 0)
        acts_all = lax.dynamic_update_index_in_dim(acts_all, own, slot, 0)

    outgoing = acts_all.reshape(micros, shards, rows, half).transpose(1, 0, 2, 3)
    arrived = lax.all_to_all(outgoing, "shard", 0, 0)
    outputs = arrived.transpose(1, 2, 0, 3).reshape(micros, rows, features)
    flat = normed_all.reshape(micros * batch, features)
    own_columns = lax.dynamic_slice(flat, (0, device * half), (micros * batch, half))
    gram = lax.dot_general(own_columns, flat, (((0,), (0,)), ((), ())), preferred_element_type=jnp.float32)
    return (outputs[None], (gram / (micros * batch))[None])


def solution(mesh):
    in_specs = (P(None, "shard", None), P("segment", None, "shard"))
    out_specs = (P("segment", None, "shard", None), P("segment", "shard", None))
    return jax.shard_map(body, mesh=mesh, in_specs=in_specs, out_specs=out_specs, check_vma=False)
```

time: 877 us -> 1050 us (1.20)
  the two profiles are of different devices: /device:TPU:1 before, /device:TPU:103 now
where the time goes in v1:
time: 1050 us; the launch traced here: 1040 us
  starting transfers between devices  560 us (53%)
  local copies, waits for them, and re-layouts  268 us (26%)
  matrix products  87.1 us (8%)
  other arithmetic  86 us (8%)
  blocking collectives  21 us (2%)
  waiting for transfers between devices  14.2 us (1%)
    ppermute x77, starting transfers between devices, move(): return lax.ppermute(value, AXES, pairs)  553 us
    dynamic_update_slice x83, local copies, waits for them, and re-layouts, body(): full = lax.dynamic_update_slice(full, part, (0, place))  102 us
    slice x40, local copies, waits for them, and re-layouts, body(): sibling_rest[:, i * block:(i + 1) * block]  61.8 us
    ppermute x48, local copies, waits for them, and re-layouts, move(): return lax.ppermute(value, AXES, pairs)  54.8 us
    dot_general x11, matrix products, body(): others = jnp.dot(inputs, swapped, preferred_element_type=jnp.float32)  43.9 us
    dot_general x11, matrix products, body(): mine = jnp.dot(inputs, kept, preferred_element_type=jnp.float32)  28.6 us
  transfers between devices with their start and end apart: 78, of which 3 were waited for; matrix products, arithmetic and copies ran while one was open for 40% of the time, Pallas kernels for 0%

profile of v1, /device:TPU:103, one launch (start us, length us, event | category | flops | bytes accessed | tf_op | source)
XLA Modules:
  0.0 1039.5 jit_solution(3712259576646332071)
XLA Ops:
  19.9 21.0 %all_to_all.10 = bf16[16,4,8,1024]{3,2,1,0:T(8,128)(2,1)S(1)} all-to-all(bf16[16,4,8,1024]{3,2,1,0:T(8,128)(2,1)S(1)} %constant_dynamic-update-slice_fusion), channel_id=1, replica_groups=mesh['segment'=8,'shard'=16] {'shard'}, dimensions={0} | all-to-all | bytes 2097152 | tf_op jit(solution)/shard_map/all_to_all | solution.py:63
  158.5 54.6 %collective-permute-start.22 = (bf16[128,1024]{0,1:T(8,128)(2,1)S(1)}, bf16[128,1024]{0,1:T(8,128)(2,1)S(1)}, u32[]{:S(2)}, u32[]{:S(2)}) collective-permute-start(bf16[128,1024]{0,1:T(8,128)(2,1)S(1)} %broadcast_select_fusion), channel_id=1, source_target_pairs={{0,8},{1,9},{2,10},{3,11},{4,12},{5,13},{6,14},{7,15},{8,0},{9,1},... | collective-permute-start | bytes 786440 | tf_op jit(solution)/shard_map/ppermute | solution.py:23
  222.7 10.5 %collective-permute-start.20 = (bf16[128,1024]{0,1:T(8,128)(2,1)S(1)}, bf16[128,1024]{0,1:T(8,128)(2,1)}, u32[]{:S(2)}, u32[]{:S(2)}) collective-permute-start(bf16[128,1024]{0,1:T(8,128)(2,1)S(1)} %broadcast_select_fusion), channel_id=1, source_target_pairs={{0,4},{1,5},{2,6},{3,7},{4,8},{5,9},{6,10},{7,11},{8,12},{9,13},{1... | collective-permute-start | bytes 786440 | tf_op jit(solution)/shard_map/ppermute | solution.py:23
  240.6 10.3 collective-permute-start.19
  264.7 10.3 collective-permute-start.23
  277.0 10.4 %collective-permute-start.69 = (bf16[128,3072]{0,1:T(8,128)(2,1)}, bf16[128,3072]{0,1:T(8,128)(2,1)}, u32[]{:S(2)}, u32[]{:S(2)}) collective-permute-start(bf16[128,3072]{0,1:T(8,128)(2,1)} %pad_maximum_fusion.9), channel_id=1, source_target_pairs={{0,1},{1,0},{2,3},{3,2},{4,5},{5,4},{6,7},{7,6},{8,9},{9,8},{10,11... | collective-permute-start | bytes 2359304 | tf_op jit(solution)/shard_map/ppermute | solution.py:23
  298.9 10.3 collective-permute-start.24
  354.0 10.3 collective-permute-start.25
  371.7 10.4 collective-permute-start.29
  383.1 10.8 %collective-permute-start.70 = (bf16[128,3072]{0,1:T(8,128)(2,1)}, bf16[128,3072]{0,1:T(8,128)(2,1)}, u32[]{:S(2)}, u32[]{:S(2)}) collective-permute-start(bf16[128,3072]{0,1:T(8,128)(2,1)} %pad_maximum_fusion.10), channel_id=1, source_target_pairs={{16,17},{17,16},{18,19},{19,18},{20,21},{21,20},{22,23},{23,22},{2... | collective-permute-start | bytes 2359304 | tf_op jit(solution)/shard_map/ppermute | solution.py:23
  418.5 16.9 %collective-permute-start.32 = (bf16[128,1024]{0,1:T(8,128)(2,1)S(1)}, bf16[128,1024]{0,1:T(8,128)(2,1)S(1)}, u32[]{:S(2)}, u32[]{:S(2)}) collective-permute-start(bf16[128,1024]{0,1:T(8,128)(2,1)S(1)} %collective-permute-done.30), channel_id=1, source_target_pairs={{32,36},{33,37},{34,38},{35,39},{36,40},{37,41},{38,42},{39,43},{4... | collective-permute-start | bytes 786440 | tf_op jit(solution)/shard_map/ppermute | solution.py:23
  441.9 10.2 collective-permute-start.33
  454.2 10.2 collective-permute-start.34
  464.4 10.9 %collective-permute-start.31 = (bf16[128,1024]{0,1:T(8,128)(2,1)S(1)}, bf16[128,1024]{0,1:T(8,128)(2,1)}, u32[]{:S(2)}, u32[]{:S(2)}) collective-permute-start(bf16[128,1024]{0,1:T(8,128)(2,1)S(1)} %collective-permute-done.30), channel_id=1, source_target_pairs={{32,33},{33,32},{34,35},{35,34},{36,37},{37,36},{38,39},{39,38},{4... | collective-permute-start | bytes 786440 | tf_op jit(solution)/shard_map/ppermute | solution.py:23
  482.7 10.4 collective-permute-start.35
  494.1 10.4 collective-permute-start.71
  519.2 10.2 collective-permute-start.36
  553.5 10.2 collective-permute-start.39
  565.9 10.2 collective-permute-start.40
  576.1 11.1 %collective-permute-start.37 = (bf16[128,1024]{0,1:T(8,128)(2,1)S(1)}, bf16[128,1024]{0,1:T(8,128)(2,1)}, u32[]{:S(2)}, u32[]{:S(2)}) collective-permute-start(bf16[128,1024]{0,1:T(8,128)(2,1)S(1)} %collective-permute-done.36), channel_id=1, source_target_pairs={{48,49},{49,48},{50,51},{51,50},{52,53},{53,52},{54,55},{55,54},{5... | collective-permute-start | bytes 786440 | tf_op jit(solution)/shard_map/ppermute | solution.py:23
  594.6 10.4 collective-permute-start.41
  605.9 10.4 collective-permute-start.72
  646.2 12.3 %collective-permute-start.44 = (bf16[128,1024]{0,1:T(8,128)(2,1)S(1)}, bf16[128,1024]{0,1:T(8,128)(2,1)S(1)}, u32[]{:S(2)}, u32[]{:S(2)}) collective-permute-start(bf16[128,1024]{0,1:T(8,128)(2,1)S(1)} %collective-permute-done.42), channel_id=1, source_target_pairs={{64,68},{65,69},{66,70},{67,71},{68,72},{69,73},{70,74},{71,75},{7... | collective-permute-start | bytes 786440 | tf_op jit(solution)/shard_map/ppermute | solution.py:23
  677.3 10.2 collective-permute-start.46
  687.5 10.2 collective-permute-start.43
  716.2 10.2 collective-permute-start.73
  741.1 10.5 %collective-permute-start.48 = (bf16[128,1024]{0,1:T(8,128)(2,1)}, bf16[128,1024]{0,1:T(8,128)(2,1)S(1)}, u32[]{:S(2)}, u32[]{:S(2)}) collective-permute-start(bf16[128,1024]{0,1:T(8,128)(2,1)} %fusion.52), channel_id=1, source_target_pairs={{64,80},{65,82},{66,81},{67,83},{68,84},{69,86},{70,85},{71,87},{7... | collective-permute-start | bytes 786440 | tf_op jit(solution)/shard_map/ppermute | solution.py:23
  764.7 10.8 %collective-permute-start.50 = (bf16[128,1024]{0,1:T(8,128)(2,1)S(1)}, bf16[128,1024]{0,1:T(8,128)(2,1)S(1)}, u32[]{:S(2)}, u32[]{:S(2)}) collective-permute-start(bf16[128,1024]{0,1:T(8,128)(2,1)S(1)} %collective-permute-done.48), channel_id=1, source_target_pairs={{80,84},{81,85},{82,86},{83,87},{84,88},{85,89},{86,90},{87,91},{8... | collective-permute-start | bytes 786440 | tf_op jit(solution)/shard_map/ppermute | solution.py:23
  776.2 10.2 collective-permute-start.51
  788.7 10.2 collective-permute-start.52
  798.9 10.2 collective-permute-start.49
  1023.3 14.6 %multiply_bitcast_fusion = f32[1,512,8192]{2,1,0:T(8,128)} fusion(bf16[512,8192]{1,0:T(8,128)(2,1)} %bitcast.274, s32[]{:T(128)S(6)} %select_n.683), kind=kOutput, calls=%fused_computation | convolution fusion | flops 4299161600 | bytes 25690116 | tf_op jit(solution)/shard_map/dot_general | solution.py:115
  (751 shorter events, 636.1 us)
Async XLA Ops:
  8.6 50.5 %collective-permute-start.4 = (bf16[4096,512]{1,0:T(8,128)(2,1)}, bf16[4096,512]{1,0:T(8,128)(2,1)}, u32[]{:S(2)}, u32[]{:S(2)}) collective-permute-start(bf16[4096,512]{1,0:T(8,128)(2,1)} %pad_maximum_fusion.1), channel_id=1, source_target_pairs={{0,1},{1,0},{2,3},{3,2},{4,5},{5,4},{6,7},{7,6},{8,9},{9,8},{10,11... | collective-permute-start | bytes 12582920 | tf_op jit(solution)/shard_map/ppermute | solution.py:23
  66.0 920.2 %collective-permute-start.66 = (bf16[128,3072]{1,0:T(8,128)(2,1)}, bf16[128,3072]{1,0:T(8,128)(2,1)}, u32[]{:S(2)}, u32[]{:S(2)}) collective-permute-start(bf16[128,3072]{1,0:T(8,128)(2,1)} %pad_maximum_fusion.6), channel_id=1, source_target_pairs={{0,1},{1,0},{2,3},{3,2},{4,5},{5,4},{6,7},{7,6},{8,9},{9,8},{10,11... | collective-permute-start | bytes 2359304 | tf_op jit(solution)/shard_map/ppermute | solution.py:23
  143.7 89.5 %collective-permute-start.68 = (bf16[128,3072]{0,1:T(8,128)(2,1)}, bf16[128,3072]{0,1:T(8,128)(2,1)}, u32[]{:S(2)}, u32[]{:S(2)}) collective-permute-start(bf16[128,3072]{0,1:T(8,128)(2,1)} %pad_maximum_fusion.8), channel_id=1, source_target_pairs={{0,1},{1,0},{2,3},{3,2},{4,5},{5,4},{6,7},{7,6},{8,9},{9,8},{10,11... | collective-permute-start | bytes 2359304 | tf_op jit(solution)/shard_map/ppermute | solution.py:23
  158.5 95.6 %collective-permute-start.22 = (bf16[128,1024]{0,1:T(8,128)(2,1)S(1)}, bf16[128,1024]{0,1:T(8,128)(2,1)S(1)}, u32[]{:S(2)}, u32[]{:S(2)}) collective-permute-start(bf16[128,1024]{0,1:T(8,128)(2,1)S(1)} %broadcast_select_fusion), channel_id=1, source_target_pairs={{0,8},{1,9},{2,10},{3,11},{4,12},{5,13},{6,14},{7,15},{8,0},{9,1},... | collective-permute-start | bytes 786440 | tf_op jit(solution)/shard_map/ppermute | solution.py:23
  213.2 40.9 %collective-permute-start.21 = (bf16[128,1024]{0,1:T(8,128)(2,1)S(1)}, bf16[128,1024]{0,1:T(8,128)(2,1)S(1)}, u32[]{:S(2)}, u32[]{:S(2)}) collective-permute-start(bf16[128,1024]{0,1:T(8,128)(2,1)S(1)} %broadcast_select_fusion), channel_id=1, source_target_pairs={{0,12},{1,13},{2,14},{3,15},{4,0},{5,1},{6,2},{7,3},{8,4},{9,5},{1... | collective-permute-start | bytes 786440 | tf_op jit(solution)/shard_map/ppermute | solution.py:23
  240.6 49.6 %collective-permute-start.19 = (bf16[128,1024]{0,1:T(8,128)(2,1)S(1)}, bf16[128,1024]{0,1:T(8,128)(2,1)}, u32[]{:S(2)}, u32[]{:S(2)}) collective-permute-start(bf16[128,1024]{0,1:T(8,128)(2,1)S(1)} %broadcast_select_fusion), channel_id=1, source_target_pairs={{0,1},{1,0},{2,3},{3,2},{4,5},{5,4},{6,7},{7,6},{8,9},{9,8},{10,11... | collective-permute-start | bytes 786440 | tf_op jit(solution)/shard_map/ppermute | solution.py:23
  277.0 33.4 %collective-permute-start.69 = (bf16[128,3072]{0,1:T(8,128)(2,1)}, bf16[128,3072]{0,1:T(8,128)(2,1)}, u32[]{:S(2)}, u32[]{:S(2)}) collective-permute-start(bf16[128,3072]{0,1:T(8,128)(2,1)} %pad_maximum_fusion.9), channel_id=1, source_target_pairs={{0,1},{1,0},{2,3},{3,2},{4,5},{5,4},{6,7},{7,6},{8,9},{9,8},{10,11... | collective-permute-start | bytes 2359304 | tf_op jit(solution)/shard_map/ppermute | solution.py:23
  322.4 41.9 %collective-permute-start.26 = (bf16[128,1024]{0,1:T(8,128)(2,1)S(1)}, bf16[128,1024]{0,1:T(8,128)(2,1)S(1)}, u32[]{:S(2)}, u32[]{:S(2)}) collective-permute-start(bf16[128,1024]{0,1:T(8,128)(2,1)S(1)} %collective-permute-done.24), channel_id=1, source_target_pairs={{16,20},{17,21},{18,22},{19,23},{20,24},{21,25},{22,26},{23,27},{2... | collective-permute-start | bytes 786440 | tf_op jit(solution)/shard_map/ppermute | solution.py:23
  354.0 43.4 %collective-permute-start.25 = (bf16[128,1024]{0,1:T(8,128)(2,1)S(1)}, bf16[128,1024]{0,1:T(8,128)(2,1)}, u32[]{:S(2)}, u32[]{:S(2)}) collective-permute-start(bf16[128,1024]{0,1:T(8,128)(2,1)S(1)} %collective-permute-done.24), channel_id=1, source_target_pairs={{16,17},{17,16},{18,19},{19,18},{20,21},{21,20},{22,23},{23,22},{2... | collective-permute-start | bytes 786440 | tf_op jit(solution)/shard_map/ppermute | solution.py:23
  371.7 34.3 %collective-permute-start.29 = (f32[128,1152]{0,1:T(8,128)}, f32[128,1152]{0,1:T(8,128)}, u32[]{:S(2)}, u32[]{:S(2)}) collective-permute-start(f32[128,1152]{0,1:T(8,128)} %pad_maximum_fusion.21), channel_id=1, source_target_pairs={{16,17},{17,16},{18,19},{19,18},{20,21},{21,20},{22,23},{23,22},{2... | collective-permute-start | bytes 1769480 | tf_op jit(solution)/shard_map/ppermute | solution.py:23
  383.1 52.4 %collective-permute-start.70 = (bf16[128,3072]{0,1:T(8,128)(2,1)}, bf16[128,3072]{0,1:T(8,128)(2,1)}, u32[]{:S(2)}, u32[]{:S(2)}) collective-permute-start(bf16[128,3072]{0,1:T(8,128)(2,1)} %pad_maximum_fusion.10), channel_id=1, source_target_pairs={{16,17},{17,16},{18,19},{19,18},{20,21},{21,20},{22,23},{23,22},{2... | collective-permute-start | bytes 2359304 | tf_op jit(solution)/shard_map/ppermute | solution.py:23
  418.5 56.8 %collective-permute-start.32 = (bf16[128,1024]{0,1:T(8,128)(2,1)S(1)}, bf16[128,1024]{0,1:T(8,128)(2,1)S(1)}, u32[]{:S(2)}, u32[]{:S(2)}) collective-permute-start(bf16[128,1024]{0,1:T(8,128)(2,1)S(1)} %collective-permute-done.30), channel_id=1, source_target_pairs={{32,36},{33,37},{34,38},{35,39},{36,40},{37,41},{38,42},{39,43},{4... | collective-permute-start | bytes 786440 | tf_op jit(solution)/shard_map/ppermute | solution.py:23
  441.9 33.5 %collective-permute-start.33 = (bf16[128,1024]{0,1:T(8,128)(2,1)S(1)}, bf16[128,1024]{0,1:T(8,128)(2,1)S(1)}, u32[]{:S(2)}, u32[]{:S(2)}) collective-permute-start(bf16[128,1024]{0,1:T(8,128)(2,1)S(1)} %collective-permute-done.30), channel_id=1, source_target_pairs={{32,44},{33,45},{34,46},{35,47},{36,32},{37,33},{38,34},{39,35},{4... | collective-permute-start | bytes 786440 | tf_op jit(solution)/shard_map/ppermute | solution.py:23
  464.4 43.6 %collective-permute-start.31 = (bf16[128,1024]{0,1:T(8,128)(2,1)S(1)}, bf16[128,1024]{0,1:T(8,128)(2,1)}, u32[]{:S(2)}, u32[]{:S(2)}) collective-permute-start(bf16[128,1024]{0,1:T(8,128)(2,1)S(1)} %collective-permute-done.30), channel_id=1, source_target_pairs={{32,33},{33,32},{34,35},{35,34},{36,37},{37,36},{38,39},{39,38},{4... | collective-permute-start | bytes 786440 | tf_op jit(solution)/shard_map/ppermute | solution.py:23
  482.7 33.9 %collective-permute-start.35 = (f32[128,1152]{0,1:T(8,128)}, f32[128,1152]{0,1:T(8,128)}, u32[]{:S(2)}, u32[]{:S(2)}) collective-permute-start(f32[128,1152]{0,1:T(8,128)} %pad_maximum_fusion.22), channel_id=1, source_target_pairs={{32,33},{33,32},{34,35},{35,34},{36,37},{37,36},{38,39},{39,38},{4... | collective-permute-start | bytes 1769480 | tf_op jit(solution)/shard_map/ppermute | solution.py:23
  494.1 36.7 %collective-permute-start.71 = (bf16[128,3072]{0,1:T(8,128)(2,1)}, bf16[128,3072]{0,1:T(8,128)(2,1)}, u32[]{:S(2)}, u32[]{:S(2)}) collective-permute-start(bf16[128,3072]{0,1:T(8,128)(2,1)} %pad_maximum_fusion.11), channel_id=1, source_target_pairs={{32,33},{33,32},{34,35},{35,34},{36,37},{37,36},{38,39},{39,38},{4... | collective-permute-start | bytes 2359304 | tf_op jit(solution)/shard_map/ppermute | solution.py:23
  542.6 44.6 %collective-permute-start.38 = (bf16[128,1024]{0,1:T(8,128)(2,1)S(1)}, bf16[128,1024]{0,1:T(8,128)(2,1)S(1)}, u32[]{:S(2)}, u32[]{:S(2)}) collective-permute-start(bf16[128,1024]{0,1:T(8,128)(2,1)S(1)} %collective-permute-done.36), channel_id=1, source_target_pairs={{48,52},{49,53},{50,54},{51,55},{52,56},{53,57},{54,58},{55,59},{5... | collective-permute-start | bytes 786440 | tf_op jit(solution)/shard_map/ppermute | solution.py:23
  553.5 33.8 %collective-permute-start.39 = (bf16[128,1024]{0,1:T(8,128)(2,1)S(1)}, bf16[128,1024]{0,1:T(8,128)(2,1)S(1)}, u32[]{:S(2)}, u32[]{:S(2)}) collective-permute-start(bf16[128,1024]{0,1:T(8,128)(2,1)S(1)} %collective-permute-done.36), channel_id=1, source_target_pairs={{48,60},{49,61},{50,62},{51,63},{52,48},{53,49},{54,50},{55,51},{5... | collective-permute-start | bytes 786440 | tf_op jit(solution)/shard_map/ppermute | solution.py:23
  576.1 43.7 %collective-permute-start.37 = (bf16[128,1024]{0,1:T(8,128)(2,1)S(1)}, bf16[128,1024]{0,1:T(8,128)(2,1)}, u32[]{:S(2)}, u32[]{:S(2)}) collective-permute-start(bf16[128,1024]{0,1:T(8,128)(2,1)S(1)} %collective-permute-done.36), channel_id=1, source_target_pairs={{48,49},{49,48},{50,51},{51,50},{52,53},{53,52},{54,55},{55,54},{5... | collective-permute-start | bytes 786440 | tf_op jit(solution)/shard_map/ppermute | solution.py:23
  594.6 33.8 %collective-permute-start.41 = (f32[128,1152]{0,1:T(8,128)}, f32[128,1152]{0,1:T(8,128)}, u32[]{:S(2)}, u32[]{:S(2)}) collective-permute-start(f32[128,1152]{0,1:T(8,128)} %pad_maximum_fusion.23), channel_id=1, source_target_pairs={{48,49},{49,48},{50,51},{51,50},{52,53},{53,52},{54,55},{55,54},{5... | collective-permute-start | bytes 1769480 | tf_op jit(solution)/shard_map/ppermute | solution.py:23
  605.9 52.6 %collective-permute-start.72 = (bf16[128,3072]{0,1:T(8,128)(2,1)}, bf16[128,3072]{0,1:T(8,128)(2,1)}, u32[]{:S(2)}, u32[]{:S(2)}) collective-permute-start(bf16[128,3072]{0,1:T(8,128)(2,1)} %pad_maximum_fusion.12), channel_id=1, source_target_pairs={{48,49},{49,48},{50,51},{51,50},{52,53},{53,52},{54,55},{55,54},{5... | collective-permute-start | bytes 2359304 | tf_op jit(solution)/shard_map/ppermute | solution.py:23
  646.2 51.5 %collective-permute-start.44 = (bf16[128,1024]{0,1:T(8,128)(2,1)S(1)}, bf16[128,1024]{0,1:T(8,128)(2,1)S(1)}, u32[]{:S(2)}, u32[]{:S(2)}) collective-permute-start(bf16[128,1024]{0,1:T(8,128)(2,1)S(1)} %collective-permute-done.42), channel_id=1, source_target_pairs={{64,68},{65,69},{66,70},{67,71},{68,72},{69,73},{70,74},{71,75},{7... | collective-permute-start | bytes 786440 | tf_op jit(solution)/shard_map/ppermute | solution.py:23
  664.9 32.8 %collective-permute-start.45 = (bf16[128,1024]{0,1:T(8,128)(2,1)S(1)}, bf16[128,1024]{0,1:T(8,128)(2,1)S(1)}, u32[]{:S(2)}, u32[]{:S(2)}) collective-permute-start(bf16[128,1024]{0,1:T(8,128)(2,1)S(1)} %collective-permute-done.42), channel_id=1, source_target_pairs={{64,76},{65,77},{66,78},{67,79},{68,64},{69,65},{70,66},{71,67},{7... | collective-permute-start | bytes 786440 | tf_op jit(solution)/shard_map/ppermute | solution.py:23
  687.5 42.5 %collective-permute-start.43 = (bf16[128,1024]{0,1:T(8,128)(2,1)S(1)}, bf16[128,1024]{0,1:T(8,128)(2,1)}, u32[]{:S(2)}, u32[]{:S(2)}) collective-permute-start(bf16[128,1024]{0,1:T(8,128)(2,1)S(1)} %collective-permute-done.42), channel_id=1, source_target_pairs={{64,65},{65,64},{66,67},{67,66},{68,69},{69,68},{70,71},{71,70},{7... | collective-permute-start | bytes 786440 | tf_op jit(solution)/shard_map/ppermute | solution.py:23
  705.1 33.4 %collective-permute-start.47 = (f32[128,1152]{0,1:T(8,128)}, f32[128,1152]{0,1:T(8,128)}, u32[]{:S(2)}, u32[]{:S(2)}) collective-permute-start(f32[128,1152]{0,1:T(8,128)} %pad_maximum_fusion.24), channel_id=1, source_target_pairs={{64,65},{65,64},{66,67},{67,66},{68,69},{69,68},{70,71},{71,70},{7... | collective-permute-start | bytes 1769480 | tf_op jit(solution)/shard_map/ppermute | solution.py:23
  716.2 36.6 %collective-permute-start.73 = (bf16[128,3072]{0,1:T(8,128)(2,1)}, bf16[128,3072]{0,1:T(8,128)(2,1)}, u32[]{:S(2)}, u32[]{:S(2)}) collective-permute-start(bf16[128,3072]{0,1:T(8,128)(2,1)} %pad_maximum_fusion.13), channel_id=1, source_target_pairs={{64,65},{65,64},{66,67},{67,66},{68,69},{69,68},{70,71},{71,70},{7... | collective-permute-start | bytes 2359304 | tf_op jit(solution)/shard_map/ppermute | solution.py:23
  764.7 44.4 %collective-permute-start.50 = (bf16[128,1024]{0,1:T(8,128)(2,1)S(1)}, bf16[128,1024]{0,1:T(8,128)(2,1)S(1)}, u32[]{:S(2)}, u32[]{:S(2)}) collective-permute-start(bf16[128,1024]{0,1:T(8,128)(2,1)S(1)} %collective-permute-done.48), channel_id=1, source_target_pairs={{80,84},{81,85},{82,86},{83,87},{84,88},{85,89},{86,90},{87,91},{8... | collective-permute-start | bytes 786440 | tf_op jit(solution)/shard_map/ppermute | solution.py:23
  776.2 32.9 %collective-permute-start.51 = (bf16[128,1024]{0,1:T(8,128)(2,1)S(1)}, bf16[128,1024]{0,1:T(8,128)(2,1)S(1)}, u32[]{:S(2)}, u32[]{:S(2)}) collective-permute-start(bf16[128,1024]{0,1:T(8,128)(2,1)S(1)} %collective-permute-done.48), channel_id=1, source_target_pairs={{80,92},{81,93},{82,94},{83,95},{84,80},{85,81},{86,82},{87,83},{8... | collective-permute-start | bytes 786440 | tf_op jit(solution)/shard_map/ppermute | solution.py:23
  798.9 42.5 %collective-permute-start.49 = (bf16[128,1024]{0,1:T(8,128)(2,1)S(1)}, bf16[128,1024]{0,1:T(8,128)(2,1)}, u32[]{:S(2)}, u32[]{:S(2)}) collective-permute-start(bf16[128,1024]{0,1:T(8,128)(2,1)S(1)} %collective-permute-done.48), channel_id=1, source_target_pairs={{80,81},{81,80},{82,83},{83,82},{84,85},{85,84},{86,87},{87,86},{8... | collective-permute-start | bytes 786440 | tf_op jit(solution)/shard_map/ppermute | solution.py:23
  816.5 33.4 %collective-permute-start.53 = (f32[128,1152]{0,1:T(8,128)}, f32[128,1152]{0,1:T(8,128)}, u32[]{:S(2)}, u32[]{:S(2)}) collective-permute-start(f32[128,1152]{0,1:T(8,128)} %pad_maximum_fusion.25), channel_id=1, source_target_pairs={{80,81},{81,80},{82,83},{83,82},{84,85},{85,84},{86,87},{87,86},{8... | collective-permute-start | bytes 1769480 | tf_op jit(solution)/shard_map/ppermute | solution.py:23
  827.6 36.6 %collective-permute-start.74 = (bf16[128,3072]{0,1:T(8,128)(2,1)}, bf16[128,3072]{0,1:T(8,128)(2,1)}, u32[]{:S(2)}, u32[]{:S(2)}) collective-permute-start(bf16[128,3072]{0,1:T(8,128)(2,1)} %pad_maximum_fusion.14), channel_id=1, source_target_pairs={{80,81},{81,80},{82,83},{83,82},{84,85},{85,84},{86,87},{87,86},{8... | collective-permute-start | bytes 2359304 | tf_op jit(solution)/shard_map/ppermute | solution.py:23
  977.1 60.9 %all-to-all-start.1 = ((bf16[16,4,8,512]{3,2,1,0:T(8,128)(2,1)}), bf16[16,4,8,512]{3,2,1,0:T(8,128)(2,1)S(1)}, u32[]{:S(2)}, u32[]{:S(2)}) async-start(bf16[16,4,8,512]{3,2,1,0:T(8,128)(2,1)} %copy.330), calls=%async_computation.1 | async-start | bytes 1048576 | tf_op jit(solution)/shard_map/all_to_all | solution.py:111
  (153 other events, 1578.8 us)

commit v2 on v1

v2 whole, which is shorter than its diff:
```python
import jax
import jax.numpy as jnp
from jax import lax
from jax.experimental import pallas as pl
from jax.experimental.pallas import tpu as pltpu
from jax.sharding import PartitionSpec as P

epsilon = 1e-05
AXES = ("segment", "shard")
SEGMENTS, ROWS, COLUMNS, CORES = 8, 4, 2, 2
STEPS = (0, 1, 3, 2)
MIB = 1 << 20


def shard_of(row, column, core):
    return (row * COLUMNS + column) * CORES + core


def move(value, target):
    pairs = []
    for s in range(SEGMENTS):
        for row in range(ROWS):
            for column in range(COLUMNS):
                for core in range(CORES):
                    t, r, c, k = target(s, row, column, core)
                    pairs.append((s * 16 + shard_of(row, column, core), t % SEGMENTS * 16 + shard_of(r % ROWS, c, k)))
    return lax.ppermute(value, AXES, pairs)


def to_sibling(value):
    return move(value, lambda s, r, c, k: (s, r, c, 1 - k))


def up_rows(value, by):
    return move(value, lambda s, r, c, k: (s, r + by, c, k))


def next_segment(value):
    return move(value, lambda s, r, c, k: (s + 1, r, k, c))


def whole(shape):
    return pl.BlockSpec(shape, lambda *_: (0,) * len(shape))


def project_kernel(a0, a1, a2, a3, kept, swapped, out):
    step = pl.program_id(0)
    half = kept.shape[1]
    for which, block in enumerate((a0, a1, a2, a3)):

        @pl.when(step == which)
        def _():
            x = block[...]
            floats = x.astype(jnp.float32)
            squares = jnp.sum(floats * floats, axis=1, keepdims=True)
            squares = jnp.broadcast_to(squares, (x.shape[0], 128))
            mine = jnp.dot(x, kept[...], preferred_element_type=jnp.float32)
            others = jnp.dot(x, swapped[...], preferred_element_type=jnp.float32)
            if which == 0:
                out[:, :half] = mine
                out[:, half : 2 * half] = others
                out[:, 2 * half :] = squares
            else:
                out[:, :half] += mine
                out[:, half : 2 * half] += others
                out[:, 2 * half :] += squares


def project(blocks, kept, swapped):
    tokens, block = blocks[0].shape
    half = kept.shape[1]
    return pl.pallas_call(
        project_kernel,
        grid=(len(blocks),),
        in_specs=[whole((tokens, block))] * 4 + [pl.BlockSpec((block, half), lambda i: (i, 0))] * 2,
        out_specs=whole((tokens, 2 * half + 128)),
        out_shape=jax.ShapeDtypeStruct((tokens, 2 * half + 128), jnp.float32),
        compiler_params=pltpu.CompilerParams(vmem_limit_bytes=24 * MIB),
        cost_estimate=pl.CostEstimate(flops=2 * tokens * 8 * half * 2 * half, bytes_accessed=9 * MIB, transcendentals=0),
        name="project",
    )(*blocks, kept, swapped)


def combine(place, own, came, held, other_held, fresh, features):
    tokens, block = held.shape

    def kernel(place, own, came, held, other_held, fresh, block_out, act_out, scale_out):
        half = block // 2
        core, column, segment = place[0], place[1], place[2]
        total = own[:, block:] + came[:, block:]
        scale = lax.rsqrt(total * (1.0 / features) + epsilon)
        scale_out[...] = scale
        factor = scale[:, :1]
        mine = (own[:, :half] + came[:, half:block]) * factor
        others = (own[:, half:block] + came[:, :half]) * factor
        residual = jnp.where(core == column, held[...], other_held[...]).astype(jnp.float32)
        low = (residual[:, :half] + jnp.where(core == 0, mine, others)).astype(jnp.bfloat16)
        high = (residual[:, half:] + jnp.where(core == 0, others, mine)).astype(jnp.bfloat16)
        act_out[...] = jnp.where(core == 0, low, high)
        if fresh is not None:
            last = segment == SEGMENTS - 1
            low = jnp.where(last, fresh[:, :half], low)
            high = jnp.where(last, fresh[:, half:], high)
        block_out[:, :half] = low
        block_out[:, half:] = high

    operands = [own, came, held, other_held]
    if fresh is not None:
        operands.append(fresh)
        run = kernel
    else:
        run = lambda p, a, b, c, d, *outs: kernel(p, a, b, c, d, None, *outs)
    return pl.pallas_call(
        run,
        in_specs=[pl.BlockSpec(memory_space=pltpu.SMEM)] + [pl.BlockSpec(memory_space=pltpu.VMEM)] * len(operands),
        out_specs=[pl.BlockSpec(memory_space=pltpu.VMEM)] * 3,
        out_shape=[
            jax.ShapeDtypeStruct((tokens, block), jnp.bfloat16),
            jax.ShapeDtypeStruct((tokens, block // 2), jnp.bfloat16),
            jax.ShapeDtypeStruct((tokens, 128), jnp.float32),
        ],
        compiler_params=pltpu.CompilerParams(vmem_limit_bytes=24 * MIB),
        cost_estimate=pl.CostEstimate(flops=8 * tokens * block, bytes_accessed=2 * MIB, transcendentals=0),
        name="combine",
    )(place, *operands)


def record(table, blocks, others, rest, scale, act, slots, features, kept_so_far):
    tokens, block = blocks[0].shape

    def kernel(table, a0, a1, a2, a3, b0, rest, scale, act, *refs):
        normed_out, acts_out = refs[-2:]
        step = pl.program_id(0)
        factor = scale[:, :1]
        for which, value in enumerate((a0, a1, a2, a3, b0)):

            @pl.when(step == which)
            def _():
                normed_out[0] = (value[...].astype(jnp.float32) * factor).astype(jnp.bfloat16)

        for which in range(3):

            @pl.when(step == 5 + which)
            def _():
                part = rest[:, which * block : (which + 1) * block]
                normed_out[0] = (part.astype(jnp.float32) * factor).astype(jnp.bfloat16)

        acts_out[0] = act[...]

    return pl.pallas_call(
        kernel,
        grid_spec=pltpu.PrefetchScalarGridSpec(
            num_scalar_prefetch=1,
            grid=(8,),
            in_specs=[whole((tokens, block))] * 5
            + [whole(rest.shape), whole(scale.shape), whole(act.shape)]
            + [pl.BlockSpec(memory_space=pl.ANY)] * len(kept_so_far),
            out_specs=[
                pl.BlockSpec((1, tokens, block), lambda i, t: (t[0], 0, t[1 + i])),
                pl.BlockSpec((1, tokens, block // 2), lambda i, t: (t[0], 0, 0)),
            ],
        ),
        out_shape=[
            jax.ShapeDtypeStruct((slots, tokens, features), jnp.bfloat16),
            jax.ShapeDtypeStruct((slots, tokens, block // 2), jnp.bfloat16),
        ],
        input_output_aliases={9: 0, 10: 1} if kept_so_far else {},
        compiler_params=pltpu.CompilerParams(vmem_limit_bytes=24 * MIB),
        cost_estimate=pl.CostEstimate(flops=2 * tokens * features, bytes_accessed=5 * MIB, transcendentals=0),
        name="record",
    )(table, *blocks, others, rest, scale, act, *kept_so_far)


def gram_of(device, flat, count, width):
    features = flat.shape[1]
    step = 1024

    def kernel(which, own, columns, out, turned):
        @pl.when(pl.program_id(0) == 0)
        def _():
            turned[...] = own[...].T

        out[...] = jnp.dot(turned[...], columns[...], preferred_element_type=jnp.float32) * (1.0 / count)

    return pl.pallas_call(
        kernel,
        grid_spec=pltpu.PrefetchScalarGridSpec(
            num_scalar_prefetch=1,
            grid=(features // step,),
            in_specs=[
                pl.BlockSpec((count, width), lambda i, d: (0, d[0])),
                pl.BlockSpec((count, step), lambda i, d: (0, i)),
            ],
            out_specs=pl.BlockSpec((width, step), lambda i, d: (0, i)),
            scratch_shapes=[pltpu.VMEM((width, count), flat.dtype)],
        ),
        out_shape=jax.ShapeDtypeStruct((width, features), jnp.float32),
        compiler_params=pltpu.CompilerParams(vmem_limit_bytes=32 * MIB),
        cost_estimate=pl.CostEstimate(flops=2 * count * width * features, bytes_accessed=26 * MIB, transcendentals=0),
        name="gram",
    )(device, flat, flat)


def body(tokens_in, weights):
    micros, rows, features = tokens_in.shape
    shards = 16
    batch = rows * shards
    block = features // 8
    half = block // 2
    device = lax.axis_index("shard")
    segment = lax.axis_index("segment")
    core = device % 2
    column = device // 2 % 2
    row = device // 4
    place = jnp.stack([core, column, segment]).astype(jnp.int32)

    pieces = weights[0].reshape(ROWS, COLUMNS, block, half)

    def rows_of(which):
        parts = [lax.dynamic_slice(pieces, ((row + ROWS - by) % ROWS, which, 0, 0), (1, 1, block, half)) for by in STEPS]
        return jnp.concatenate([p[0, 0] for p in parts], axis=0)

    swapped = to_sibling(rows_of(1 - core))
    kept = rows_of(core)

    split = tokens_in.reshape(micros, rows, ROWS, COLUMNS, block)
    outgoing = jnp.stack(
        [
            jnp.concatenate([split[:1, :, r, k], split[1:, :, r, c]], axis=0)
            for r in range(ROWS)
            for c in range(COLUMNS)
            for k in range(CORES)
        ]
    )
    arrived = lax.all_to_all(outgoing, "shard", 0, 0)
    tokens = arrived.transpose(1, 0, 2, 3).reshape(micros, batch, block)

    stores = ()
    order = [(row + ROWS - by) % ROWS * COLUMNS for by in STEPS]
    order = [o + core for o in order] + [o + 1 - core for o in order]
    held = tokens[0]
    for tick in range(micros + SEGMENTS - 1):
        if tick > 0:
            held = next_segment(chip_block)
        blocks = [held] + [up_rows(held, by) for by in STEPS[1:]]
        other_held = to_sibling(held)
        own = project(blocks, kept, swapped)
        came = to_sibling(own)
        fresh = tokens[tick + 1] if tick + 1 < micros else None
        chip_block, act, scale = combine(place, own, came, held, other_held, fresh, features)
        rest = to_sibling(jnp.concatenate(blocks[1:], axis=1))
        group = tick - segment
        slot = jnp.where((group >= 0) & (group < micros), group, micros)
        table = jnp.stack([slot] + order).astype(jnp.int32)
        stores = record(table, blocks, other_held, rest, scale, act, micros + 1, features, stores)
    normed_all, acts_all = stores

    outgoing = acts_all[:micros].reshape(micros, shards, rows, half).transpose(1, 0, 2, 3)
    arrived = lax.all_to_all(outgoing, "shard", 0, 0)
    outputs = arrived.transpose(1, 2, 0, 3).reshape(micros, rows, features)
    flat = normed_all.reshape((micros + 1) * batch, features)
    gram = gram_of(device.reshape(1).astype(jnp.int32), flat, micros * batch, half)
    return (outputs[None], gram[None])


def solution(mesh):
    in_specs = (P(None, "shard", None), P("segment", None, "shard"))
    out_specs = (P("segment", None, "shard", None), P("segment", "shard", None))
    return jax.shard_map(body, mesh=mesh, in_specs=in_specs, out_specs=out_specs, check_vma=False)
```

time: 1050 us -> 450 us (0.43)
  the two profiles are of different devices: /device:TPU:103 before, /device:TPU:1 now
where the time goes in v2:
time: 450 us; the launch traced here: 441 us
  waiting for transfers between devices  251 us (56%)
  Pallas kernels  67 us (15%)
  starting transfers between devices  58.7 us (13%)
  local copies, waits for them, and re-layouts  34.9 us (8%)
  blocking collectives  21.3 us (5%)
    ppermute x77, waiting for transfers between devices, move(): return lax.ppermute(value, AXES, pairs)  251 us
    ppermute x77, starting transfers between devices, move(): return lax.ppermute(value, AXES, pairs)  54 us
    pallas_call x11, Pallas kernels, record(): pl.pallas_call(kernel, grid_spec=pltpu.PrefetchScalarGridSpec(num_scalar_...  26.4 us
    unnamed x308, local copies, waits for them, and re-layouts  22.9 us
    pallas_call x11, Pallas kernels, project(): pl.pallas_call(project_kernel, grid=(len(blocks),), in_specs=[whole((toke...  21.8 us
    all_to_all x1, blocking collectives, body(): arrived = lax.all_to_all(outgoing, 'shard', 0, 0)  21.3 us
    pallas_call x1, Pallas kernels, gram_of(): pl.pallas_call(kernel, grid_spec=pltpu.PrefetchScalarGridSpec(num_scalar_...  9.46 us
    pallas_call x11, Pallas kernels, combine(): pl.pallas_call(run, in_specs=[pl.BlockSpec(memory_space=pltpu.SMEM)] + [p...  9.46 us
  transfers between devices with their start and end apart: 78, of which 52 were waited for; matrix products, arithmetic and copies ran while one was open for 2% of the time, Pallas kernels for 9%

profile of v2, /device:TPU:1, one launch (start us, length us, event | category | flops | bytes accessed | tf_op | source)
XLA Modules:
  0.0 440.8 jit_solution(12428674381838510628)
XLA Ops:
  0.7 4.3 dynamic-slice_bitcast_fusion.3
  7.2 21.3 %all_to_all.10 = bf16[16,4,8,1024]{3,2,1,0:T(8,128)(2,1)S(1)} all-to-all(bf16[16,4,8,1024]{3,2,1,0:T(8,128)(2,1)S(1)} %fusion.3), channel_id=1, replica_groups=mesh['segment'=8,'shard'=16] {'shard'}, dimensions={0} | all-to-all | bytes 2097152 | tf_op jit(solution)/shard_map/all_to_all | solution.py:235
  31.7 5.8 %collective-permute-done.a1 = bf16[128,1024]{1,0:T(8,128)(2,1)S(1)} collective-permute-done((bf16[128,1024]{1,0:T(8,128)(2,1)S(1)}, bf16[128,1024]{1,0:T(8,128)(2,1)S(1)}, u32[]{:S(2)}, u32[]{:S(2)}) %collective-permute-start) | collective-permute-done | bytes 262176 | tf_op jit(solution)/shard_map/ppermute | solution.py:27
  52.5 10.2 %collective-permute-done.6.a0.held = bf16[128,1024]{1,0:T(8,128)(2,1)S(1)} collective-permute-done((bf16[128,1024]{1,0:T(8,128)(2,1)S(1)}, bf16[128,1024]{1,0:T(8,128)(2,1)S(1)}, u32[]{:S(2)}, u32[]{:S(2)}) %collective-permute-start.6) | collective-permute-done | bytes 262176 | tf_op jit(solution)/shard_map/ppermute | solution.py:27
  66.6 4.6 %collective-permute-done.7.a1 = bf16[128,1024]{1,0:T(8,128)(2,1)S(1)} collective-permute-done((bf16[128,1024]{1,0:T(8,128)(2,1)S(1)}, bf16[128,1024]{1,0:T(8,128)(2,1)S(1)}, u32[]{:S(2)}, u32[]{:S(2)}) %collective-permute-start.7) | collective-permute-done | bytes 262176 | tf_op jit(solution)/shard_map/ppermute | solution.py:27
  71.2 4.7 %collective-permute-done.8.a2 = bf16[128,1024]{1,0:T(8,128)(2,1)S(1)} collective-permute-done((bf16[128,1024]{1,0:T(8,128)(2,1)S(1)}, bf16[128,1024]{1,0:T(8,128)(2,1)S(1)}, u32[]{:S(2)}, u32[]{:S(2)}) %collective-permute-start.8) | collective-permute-done | bytes 262176 | tf_op jit(solution)/shard_map/ppermute | solution.py:27
  86.8 11.9 %collective-permute-done.12.a0.held = bf16[128,1024]{1,0:T(8,128)(2,1)S(1)} collective-permute-done((bf16[128,1024]{1,0:T(8,128)(2,1)S(1)}, bf16[128,1024]{1,0:T(8,128)(2,1)S(1)}, u32[]{:S(2)}, u32[]{:S(2)}) %collective-permute-start.12) | collective-permute-done | bytes 262176 | tf_op jit(solution)/shard_map/ppermute | solution.py:27
  101.8 6.1 %collective-permute-done.13.a1 = bf16[128,1024]{1,0:T(8,128)(2,1)S(1)} collective-permute-done((bf16[128,1024]{1,0:T(8,128)(2,1)S(1)}, bf16[128,1024]{1,0:T(8,128)(2,1)S(1)}, u32[]{:S(2)}, u32[]{:S(2)}) %collective-permute-start.13) | collective-permute-done | bytes 262176 | tf_op jit(solution)/shard_map/ppermute | solution.py:27
  107.9 4.3 collective-permute-done.14.a2
  119.2 11.9 %collective-permute-done.18.a0.c = bf16[128,1024]{1,0:T(8,128)(2,1)S(1)} collective-permute-done((bf16[128,1024]{1,0:T(8,128)(2,1)S(1)}, bf16[128,1024]{1,0:T(8,128)(2,1)S(1)}, u32[]{:S(2)}, u32[]{:S(2)}) %collective-permute-start.18) | collective-permute-done | bytes 262176 | tf_op jit(solution)/shard_map/ppermute | solution.py:27
  134.9 4.7 %collective-permute-done.19.a1 = bf16[128,1024]{1,0:T(8,128)(2,1)S(1)} collective-permute-done((bf16[128,1024]{1,0:T(8,128)(2,1)S(1)}, bf16[128,1024]{1,0:T(8,128)(2,1)S(1)}, u32[]{:S(2)}, u32[]{:S(2)}) %collective-permute-start.19) | collective-permute-done | bytes 262176 | tf_op jit(solution)/shard_map/ppermute | solution.py:27
  139.6 5.0 %collective-permute-done.20.a2 = bf16[128,1024]{1,0:T(8,128)(2,1)S(1)} collective-permute-done((bf16[128,1024]{1,0:T(8,128)(2,1)S(1)}, bf16[128,1024]{1,0:T(8,128)(2,1)S(1)}, u32[]{:S(2)}, u32[]{:S(2)}) %collective-permute-start.20) | collective-permute-done | bytes 262176 | tf_op jit(solution)/shard_map/ppermute | solution.py:27
  151.0 11.9 %collective-permute-done.24.a0.c = bf16[128,1024]{1,0:T(8,128)(2,1)S(1)} collective-permute-done((bf16[128,1024]{1,0:T(8,128)(2,1)S(1)}, bf16[128,1024]{1,0:T(8,128)(2,1)S(1)}, u32[]{:S(2)}, u32[]{:S(2)}) %collective-permute-start.24) | collective-permute-done | bytes 262176 | tf_op jit(solution)/shard_map/ppermute | solution.py:27
  166.0 6.1 %collective-permute-done.25.a1 = bf16[128,1024]{1,0:T(8,128)(2,1)S(1)} collective-permute-done((bf16[128,1024]{1,0:T(8,128)(2,1)S(1)}, bf16[128,1024]{1,0:T(8,128)(2,1)S(1)}, u32[]{:S(2)}, u32[]{:S(2)}) %collective-permute-start.25) | collective-permute-done | bytes 262176 | tf_op jit(solution)/shard_map/ppermute | solution.py:27
  182.2 11.9 %collective-permute-done.30.a0.c = bf16[128,1024]{1,0:T(8,128)(2,1)S(1)} collective-permute-done((bf16[128,1024]{1,0:T(8,128)(2,1)S(1)}, bf16[128,1024]{1,0:T(8,128)(2,1)S(1)}, u32[]{:S(2)}, u32[]{:S(2)}) %collective-permute-start.30) | collective-permute-done | bytes 262176 | tf_op jit(solution)/shard_map/ppermute | solution.py:27
  197.9 4.7 %collective-permute-done.31.a1 = bf16[128,1024]{1,0:T(8,128)(2,1)S(1)} collective-permute-done((bf16[128,1024]{1,0:T(8,128)(2,1)S(1)}, bf16[128,1024]{1,0:T(8,128)(2,1)S(1)}, u32[]{:S(2)}, u32[]{:S(2)}) %collective-permute-start.31) | collective-permute-done | bytes 262176 | tf_op jit(solution)/shard_map/ppermute | solution.py:27
  202.6 5.0 %collective-permute-done.32.a2 = bf16[128,1024]{1,0:T(8,128)(2,1)S(1)} collective-permute-done((bf16[128,1024]{1,0:T(8,128)(2,1)S(1)}, bf16[128,1024]{1,0:T(8,128)(2,1)S(1)}, u32[]{:S(2)}, u32[]{:S(2)}) %collective-permute-start.32) | collective-permute-done | bytes 262176 | tf_op jit(solution)/shard_map/ppermute | solution.py:27
  214.0 11.9 %collective-permute-done.36.a0.c = bf16[128,1024]{1,0:T(8,128)(2,1)S(1)} collective-permute-done((bf16[128,1024]{1,0:T(8,128)(2,1)S(1)}, bf16[128,1024]{1,0:T(8,128)(2,1)S(1)}, u32[]{:S(2)}, u32[]{:S(2)}) %collective-permute-start.36) | collective-permute-done | bytes 262176 | tf_op jit(solution)/shard_map/ppermute | solution.py:27
  229.2 6.0 %collective-permute-done.37.a1 = bf16[128,1024]{1,0:T(8,128)(2,1)S(1)} collective-permute-done((bf16[128,1024]{1,0:T(8,128)(2,1)S(1)}, bf16[128,1024]{1,0:T(8,128)(2,1)S(1)}, u32[]{:S(2)}, u32[]{:S(2)}) %collective-permute-start.37) | collective-permute-done | bytes 262176 | tf_op jit(solution)/shard_map/ppermute | solution.py:27
  245.2 11.9 %collective-permute-done.42.a0.c = bf16[128,1024]{1,0:T(8,128)(2,1)S(1)} collective-permute-done((bf16[128,1024]{1,0:T(8,128)(2,1)S(1)}, bf16[128,1024]{1,0:T(8,128)(2,1)S(1)}, u32[]{:S(2)}, u32[]{:S(2)}) %collective-permute-start.42) | collective-permute-done | bytes 262176 | tf_op jit(solution)/shard_map/ppermute | solution.py:27
  260.9 4.7 %collective-permute-done.43.a1 = bf16[128,1024]{1,0:T(8,128)(2,1)S(1)} collective-permute-done((bf16[128,1024]{1,0:T(8,128)(2,1)S(1)}, bf16[128,1024]{1,0:T(8,128)(2,1)S(1)}, u32[]{:S(2)}, u32[]{:S(2)}) %collective-permute-start.43) | collective-permute-done | bytes 262176 | tf_op jit(solution)/shard_map/ppermute | solution.py:27
  265.6 5.0 %collective-permute-done.44.a2 = bf16[128,1024]{1,0:T(8,128)(2,1)S(1)} collective-permute-done((bf16[128,1024]{1,0:T(8,128)(2,1)S(1)}, bf16[128,1024]{1,0:T(8,128)(2,1)S(1)}, u32[]{:S(2)}, u32[]{:S(2)}) %collective-permute-start.44) | collective-permute-done | bytes 262176 | tf_op jit(solution)/shard_map/ppermute | solution.py:27
  277.0 11.9 %collective-permute-done.48.a0.c = bf16[128,1024]{1,0:T(8,128)(2,1)S(1)} collective-permute-done((bf16[128,1024]{1,0:T(8,128)(2,1)S(1)}, bf16[128,1024]{1,0:T(8,128)(2,1)S(1)}, u32[]{:S(2)}, u32[]{:S(2)}) %collective-permute-start.48) | collective-permute-done | bytes 262176 | tf_op jit(solution)/shard_map/ppermute | solution.py:27
  292.0 6.1 %collective-permute-done.49.a1 = bf16[128,1024]{1,0:T(8,128)(2,1)S(1)} collective-permute-done((bf16[128,1024]{1,0:T(8,128)(2,1)S(1)}, bf16[128,1024]{1,0:T(8,128)(2,1)S(1)}, u32[]{:S(2)}, u32[]{:S(2)}) %collective-permute-start.49) | collective-permute-done | bytes 262176 | tf_op jit(solution)/shard_map/ppermute | solution.py:27
  309.4 11.8 %collective-permute-done.54.a0.c = bf16[128,1024]{1,0:T(8,128)(2,1)S(1)} collective-permute-done((bf16[128,1024]{1,0:T(8,128)(2,1)S(1)}, bf16[128,1024]{1,0:T(8,128)(2,1)S(1)}, u32[]{:S(2)}, u32[]{:S(2)}) %collective-permute-start.54) | collective-permute-done | bytes 262176 | tf_op jit(solution)/shard_map/ppermute | solution.py:27
  325.1 4.6 %collective-permute-done.55.a1 = bf16[128,1024]{1,0:T(8,128)(2,1)S(1)} collective-permute-done((bf16[128,1024]{1,0:T(8,128)(2,1)S(1)}, bf16[128,1024]{1,0:T(8,128)(2,1)S(1)}, u32[]{:S(2)}, u32[]{:S(2)}) %collective-permute-start.55) | collective-permute-done | bytes 262176 | tf_op jit(solution)/shard_map/ppermute | solution.py:27
  329.9 4.8 %collective-permute-done.56.a2 = bf16[128,1024]{1,0:T(8,128)(2,1)S(1)} collective-permute-done((bf16[128,1024]{1,0:T(8,128)(2,1)S(1)}, bf16[128,1024]{1,0:T(8,128)(2,1)S(1)}, u32[]{:S(2)}, u32[]{:S(2)}) %collective-permute-start.56) | collective-permute-done | bytes 262176 | tf_op jit(solution)/shard_map/ppermute | solution.py:27
  345.5 9.7 %collective-permute-done.60.a0.c = bf16[128,1024]{1,0:T(8,128)(2,1)} collective-permute-done((bf16[128,1024]{1,0:T(8,128)(2,1)S(1)}, bf16[128,1024]{1,0:T(8,128)(2,1)}, u32[]{:S(2)}, u32[]{:S(2)}) %collective-permute-start.60) | collective-permute-done | bytes 262176 | tf_op jit(solution)/shard_map/ppermute | solution.py:27
  359.3 5.3 %collective-permute-done.61.a1 = bf16[128,1024]{1,0:T(8,128)(2,1)S(1)} collective-permute-done((bf16[128,1024]{1,0:T(8,128)(2,1)}, bf16[128,1024]{1,0:T(8,128)(2,1)S(1)}, u32[]{:S(2)}, u32[]{:S(2)}) %collective-permute-start.61) | collective-permute-done | bytes 262176 | tf_op jit(solution)/shard_map/ppermute | solution.py:27
  364.6 4.7 %collective-permute-done.62.a2 = bf16[128,1024]{1,0:T(8,128)(2,1)S(1)} collective-permute-done((bf16[128,1024]{1,0:T(8,128)(2,1)}, bf16[128,1024]{1,0:T(8,128)(2,1)S(1)}, u32[]{:S(2)}, u32[]{:S(2)}) %collective-permute-start.62) | collective-permute-done | bytes 262176 | tf_op jit(solution)/shard_map/ppermute | solution.py:27
  420.9 4.7 %all-to-all-start.1 = ((bf16[16,4,8,512]{3,2,1,0:T(8,128)(2,1)}), bf16[16,4,8,512]{3,2,1,0:T(8,128)(2,1)S(1)}, u32[]{:S(2)}, u32[]{:S(2)}) async-start(bf16[16,4,8,512]{3,2,1,0:T(8,128)(2,1)} %copy_bitcast_fusion), calls=%async_computation.1 | async-start | bytes 1048576 | tf_op jit(solution)/shard_map/all_to_all | solution.py:259
  429.6 9.5 %gram.1 = f32[512,8192]{1,0:T(8,128)} custom-call(s32[1]{0:T(128)} %bitcast.72.which, bf16[640,8192]{1,0:T(8,128)(2,1)S(1)} %bitcast.156, bf16[640,8192]{1,0:T(8,128)(2,1)S(1)} %bitcast.157), custom_call_target="tpu_custom_call" | custom-call | flops 4294967296 | bytes 27262976 | tf_op jit(solution)/shard_map/gram/pallas_call | solution.py:185
  (515 shorter events, 190.4 us)
Async XLA Ops:
  5.4 35.9 %collective-permute-start.3 = (bf16[4096,512]{1,0:T(8,128)(2,1)S(1)}, bf16[4096,512]{1,0:T(8,128)(2,1)S(1)}, u32[]{:S(2)}, u32[]{:S(2)}) collective-permute-start(bf16[4096,512]{1,0:T(8,128)(2,1)S(1)} %pad_maximum_fusion.1), channel_id=1, source_target_pairs={{0,1},{1,0},{2,3},{3,2},{4,5},{5,4},{6,7},{7,6},{8,9},{9,8},{10,11... | collective-permute-start | bytes 12582920 | tf_op jit(solution)/shard_map/ppermute | solution.py:27
  49.7 13.1 %collective-permute-start.6 = (bf16[128,1024]{1,0:T(8,128)(2,1)S(1)}, bf16[128,1024]{1,0:T(8,128)(2,1)S(1)}, u32[]{:S(2)}, u32[]{:S(2)}) collective-permute-start(bf16[128,1024]{1,0:T(8,128)(2,1)S(1)} %get-tuple-element.56), channel_id=1, source_target_pairs={{0,16},{1,18},{2,17},{3,19},{4,20},{5,22},{6,21},{7,23},{8,24},{9,... | collective-permute-start | bytes 786440 | tf_op jit(solution)/shard_map/ppermute | solution.py:27
  63.3 12.6 %collective-permute-start.8 = (bf16[128,1024]{1,0:T(8,128)(2,1)S(1)}, bf16[128,1024]{1,0:T(8,128)(2,1)S(1)}, u32[]{:S(2)}, u32[]{:S(2)}) collective-permute-start(bf16[128,1024]{1,0:T(8,128)(2,1)S(1)} %collective-permute-done.6.a0.held), channel_id=1, source_target_pairs={{0,12},{1,13},{2,14},{3,15},{4,0},{5,1},{6,2},{7,3},{8,4},{9,5},{1... | collective-permute-start | bytes 786440 | tf_op jit(solution)/shard_map/ppermute | solution.py:27
  86.7 12.0 %collective-permute-start.12 = (bf16[128,1024]{1,0:T(8,128)(2,1)S(1)}, bf16[128,1024]{1,0:T(8,128)(2,1)S(1)}, u32[]{:S(2)}, u32[]{:S(2)}) collective-permute-start(bf16[128,1024]{1,0:T(8,128)(2,1)S(1)} %get-tuple-element.57), channel_id=1, source_target_pairs={{0,16},{1,18},{2,17},{3,19},{4,20},{5,22},{6,21},{7,23},{8,24},{9,... | collective-permute-start | bytes 786440 | tf_op jit(solution)/shard_map/ppermute | solution.py:27
  99.8 12.3 %collective-permute-start.14 = (bf16[128,1024]{1,0:T(8,128)(2,1)S(1)}, bf16[128,1024]{1,0:T(8,128)(2,1)S(1)}, u32[]{:S(2)}, u32[]{:S(2)}) collective-permute-start(bf16[128,1024]{1,0:T(8,128)(2,1)S(1)} %collective-permute-done.12.a0.held), channel_id=1, source_target_pairs={{0,12},{1,13},{2,14},{3,15},{4,0},{5,1},{6,2},{7,3},{8,4},{9,5},{1... | collective-permute-start | bytes 786440 | tf_op jit(solution)/shard_map/ppermute | solution.py:27
  132.2 12.3 %collective-permute-start.20 = (bf16[128,1024]{1,0:T(8,128)(2,1)S(1)}, bf16[128,1024]{1,0:T(8,128)(2,1)S(1)}, u32[]{:S(2)}, u32[]{:S(2)}) collective-permute-start(bf16[128,1024]{1,0:T(8,128)(2,1)S(1)} %collective-permute-done.18.a0.c), channel_id=1, source_target_pairs={{0,12},{1,13},{2,14},{3,15},{4,0},{5,1},{6,2},{7,3},{8,4},{9,5},{1... | collective-permute-start | bytes 786440 | tf_op jit(solution)/shard_map/ppermute | solution.py:27
  133.8 12.0 %collective-permute-start.21 = (bf16[128,1024]{1,0:T(8,128)(2,1)S(1)}, bf16[128,1024]{1,0:T(8,128)(2,1)S(1)}, u32[]{:S(2)}, u32[]{:S(2)}) collective-permute-start(bf16[128,1024]{1,0:T(8,128)(2,1)S(1)} %collective-permute-done.18.a0.c), channel_id=1, source_target_pairs={{0,8},{1,9},{2,10},{3,11},{4,12},{5,13},{6,14},{7,15},{8,0},{9,1},... | collective-permute-start | bytes 786440 | tf_op jit(solution)/shard_map/ppermute | solution.py:27
  164.1 12.3 %collective-permute-start.26 = (bf16[128,1024]{1,0:T(8,128)(2,1)S(1)}, bf16[128,1024]{1,0:T(8,128)(2,1)S(1)}, u32[]{:S(2)}, u32[]{:S(2)}) collective-permute-start(bf16[128,1024]{1,0:T(8,128)(2,1)S(1)} %collective-permute-done.24.a0.c), channel_id=1, source_target_pairs={{0,12},{1,13},{2,14},{3,15},{4,0},{5,1},{6,2},{7,3},{8,4},{9,5},{1... | collective-permute-start | bytes 786440 | tf_op jit(solution)/shard_map/ppermute | solution.py:27
  195.3 12.3 %collective-permute-start.32 = (bf16[128,1024]{1,0:T(8,128)(2,1)S(1)}, bf16[128,1024]{1,0:T(8,128)(2,1)S(1)}, u32[]{:S(2)}, u32[]{:S(2)}) collective-permute-start(bf16[128,1024]{1,0:T(8,128)(2,1)S(1)} %collective-permute-done.30.a0.c), channel_id=1, source_target_pairs={{0,12},{1,13},{2,14},{3,15},{4,0},{5,1},{6,2},{7,3},{8,4},{9,5},{1... | collective-permute-start | bytes 786440 | tf_op jit(solution)/shard_map/ppermute | solution.py:27
  196.8 12.0 %collective-permute-start.33 = (bf16[128,1024]{1,0:T(8,128)(2,1)S(1)}, bf16[128,1024]{1,0:T(8,128)(2,1)S(1)}, u32[]{:S(2)}, u32[]{:S(2)}) collective-permute-start(bf16[128,1024]{1,0:T(8,128)(2,1)S(1)} %collective-permute-done.30.a0.c), channel_id=1, source_target_pairs={{0,8},{1,9},{2,10},{3,11},{4,12},{5,13},{6,14},{7,15},{8,0},{9,1},... | collective-permute-start | bytes 786440 | tf_op jit(solution)/shard_map/ppermute | solution.py:27
  227.1 12.3 %collective-permute-start.38 = (bf16[128,1024]{1,0:T(8,128)(2,1)S(1)}, bf16[128,1024]{1,0:T(8,128)(2,1)S(1)}, u32[]{:S(2)}, u32[]{:S(2)}) collective-permute-start(bf16[128,1024]{1,0:T(8,128)(2,1)S(1)} %collective-permute-done.36.a0.c), channel_id=1, source_target_pairs={{0,12},{1,13},{2,14},{3,15},{4,0},{5,1},{6,2},{7,3},{8,4},{9,5},{1... | collective-permute-start | bytes 786440 | tf_op jit(solution)/shard_map/ppermute | solution.py:27
  245.1 12.0 %collective-permute-start.42 = (bf16[128,1024]{1,0:T(8,128)(2,1)S(1)}, bf16[128,1024]{1,0:T(8,128)(2,1)S(1)}, u32[]{:S(2)}, u32[]{:S(2)}) collective-permute-start(bf16[128,1024]{1,0:T(8,128)(2,1)S(1)} %get-tuple-element.62), channel_id=1, source_target_pairs={{0,16},{1,18},{2,17},{3,19},{4,20},{5,22},{6,21},{7,23},{8,24},{9,... | collective-permute-start | bytes 786440 | tf_op jit(solution)/shard_map/ppermute | solution.py:27
  258.2 12.3 %collective-permute-start.44 = (bf16[128,1024]{1,0:T(8,128)(2,1)S(1)}, bf16[128,1024]{1,0:T(8,128)(2,1)S(1)}, u32[]{:S(2)}, u32[]{:S(2)}) collective-permute-start(bf16[128,1024]{1,0:T(8,128)(2,1)S(1)} %collective-permute-done.42.a0.c), channel_id=1, source_target_pairs={{0,12},{1,13},{2,14},{3,15},{4,0},{5,1},{6,2},{7,3},{8,4},{9,5},{1... | collective-permute-start | bytes 786440 | tf_op jit(solution)/shard_map/ppermute | solution.py:27
  259.8 12.0 %collective-permute-start.45 = (bf16[128,1024]{1,0:T(8,128)(2,1)S(1)}, bf16[128,1024]{1,0:T(8,128)(2,1)S(1)}, u32[]{:S(2)}, u32[]{:S(2)}) collective-permute-start(bf16[128,1024]{1,0:T(8,128)(2,1)S(1)} %collective-permute-done.42.a0.c), channel_id=1, source_target_pairs={{0,8},{1,9},{2,10},{3,11},{4,12},{5,13},{6,14},{7,15},{8,0},{9,1},... | collective-permute-start | bytes 786440 | tf_op jit(solution)/shard_map/ppermute | solution.py:27
  290.1 12.3 %collective-permute-start.50 = (bf16[128,1024]{1,0:T(8,128)(2,1)S(1)}, bf16[128,1024]{1,0:T(8,128)(2,1)S(1)}, u32[]{:S(2)}, u32[]{:S(2)}) collective-permute-start(bf16[128,1024]{1,0:T(8,128)(2,1)S(1)} %collective-permute-done.48.a0.c), channel_id=1, source_target_pairs={{0,12},{1,13},{2,14},{3,15},{4,0},{5,1},{6,2},{7,3},{8,4},{9,5},{1... | collective-permute-start | bytes 786440 | tf_op jit(solution)/shard_map/ppermute | solution.py:27
  305.0 38.0 %collective-permute-start.76 = (bf16[128,3072]{1,0:T(8,128)(2,1)S(1)}, bf16[128,3072]{1,0:T(8,128)(2,1)S(1)}, u32[]{:S(2)}, u32[]{:S(2)}) collective-permute-start(bf16[128,3072]{1,0:T(8,128)(2,1)S(1)} %pad_maximum_fusion.12), channel_id=1, source_target_pairs={{0,1},{1,0},{2,3},{3,2},{4,5},{5,4},{6,7},{7,6},{8,9},{9,8},{10,11... | collective-permute-start | bytes 2359304 | tf_op jit(solution)/shard_map/ppermute | solution.py:27
  305.7 37.4 %collective-permute-start.75 = (bf16[128,3072]{1,0:T(8,128)(2,1)S(1)}, bf16[128,3072]{1,0:T(8,128)(2,1)S(1)}, u32[]{:S(2)}, u32[]{:S(2)}) collective-permute-start(bf16[128,3072]{1,0:T(8,128)(2,1)S(1)} %pad_maximum_fusion.11), channel_id=1, source_target_pairs={{0,1},{1,0},{2,3},{3,2},{4,5},{5,4},{6,7},{7,6},{8,9},{9,8},{10,11... | collective-permute-start | bytes 2359304 | tf_op jit(solution)/shard_map/ppermute | solution.py:27
  322.3 12.3 %collective-permute-start.56 = (bf16[128,1024]{1,0:T(8,128)(2,1)S(1)}, bf16[128,1024]{1,0:T(8,128)(2,1)S(1)}, u32[]{:S(2)}, u32[]{:S(2)}) collective-permute-start(bf16[128,1024]{1,0:T(8,128)(2,1)S(1)} %collective-permute-done.54.a0.c), channel_id=1, source_target_pairs={{0,12},{1,13},{2,14},{3,15},{4,0},{5,1},{6,2},{7,3},{8,4},{9,5},{1... | collective-permute-start | bytes 786440 | tf_op jit(solution)/shard_map/ppermute | solution.py:27
  323.9 12.0 %collective-permute-start.57 = (bf16[128,1024]{1,0:T(8,128)(2,1)S(1)}, bf16[128,1024]{1,0:T(8,128)(2,1)S(1)}, u32[]{:S(2)}, u32[]{:S(2)}) collective-permute-start(bf16[128,1024]{1,0:T(8,128)(2,1)S(1)} %collective-permute-done.54.a0.c), channel_id=1, source_target_pairs={{0,8},{1,9},{2,10},{3,11},{4,12},{5,13},{6,14},{7,15},{8,0},{9,1},... | collective-permute-start | bytes 786440 | tf_op jit(solution)/shard_map/ppermute | solution.py:27
  329.7 14.7 %collective-permute-start.74 = (bf16[128,3072]{1,0:T(8,128)(2,1)S(1)}, bf16[128,3072]{1,0:T(8,128)(2,1)S(1)}, u32[]{:S(2)}, u32[]{:S(2)}) collective-permute-start(bf16[128,3072]{1,0:T(8,128)(2,1)S(1)} %pad_maximum_fusion.10), channel_id=1, source_target_pairs={{0,1},{1,0},{2,3},{3,2},{4,5},{5,4},{6,7},{7,6},{8,9},{9,8},{10,11... | collective-permute-start | bytes 2359304 | tf_op jit(solution)/shard_map/ppermute | solution.py:27
  340.3 16.0 %collective-permute-start.73 = (bf16[128,3072]{1,0:T(8,128)(2,1)S(1)}, bf16[128,3072]{1,0:T(8,128)(2,1)S(1)}, u32[]{:S(2)}, u32[]{:S(2)}) collective-permute-start(bf16[128,3072]{1,0:T(8,128)(2,1)S(1)} %pad_maximum_fusion.9), channel_id=1, source_target_pairs={{0,1},{1,0},{2,3},{3,2},{4,5},{5,4},{6,7},{7,6},{8,9},{9,8},{10,11... | collective-permute-start | bytes 2359304 | tf_op jit(solution)/shard_map/ppermute | solution.py:27
  340.5 17.4 %collective-permute-start.72 = (bf16[128,3072]{1,0:T(8,128)(2,1)S(1)}, bf16[128,3072]{1,0:T(8,128)(2,1)S(1)}, u32[]{:S(2)}, u32[]{:S(2)}) collective-permute-start(bf16[128,3072]{1,0:T(8,128)(2,1)S(1)} %pad_maximum_fusion.8), channel_id=1, source_target_pairs={{0,1},{1,0},{2,3},{3,2},{4,5},{5,4},{6,7},{7,6},{8,9},{9,8},{10,11... | collective-permute-start | bytes 2359304 | tf_op jit(solution)/shard_map/ppermute | solution.py:27
  343.0 27.7 %collective-permute-start.71 = (bf16[128,3072]{1,0:T(8,128)(2,1)S(1)}, bf16[128,3072]{1,0:T(8,128)(2,1)S(1)}, u32[]{:S(2)}, u32[]{:S(2)}) collective-permute-start(bf16[128,3072]{1,0:T(8,128)(2,1)S(1)} %pad_maximum_fusion.7), channel_id=1, source_target_pairs={{0,1},{1,0},{2,3},{3,2},{4,5},{5,4},{6,7},{7,6},{8,9},{9,8},{10,11... | collective-permute-start | bytes 2359304 | tf_op jit(solution)/shard_map/ppermute | solution.py:27
  343.2 12.0 %collective-permute-start.60 = (bf16[128,1024]{1,0:T(8,128)(2,1)S(1)}, bf16[128,1024]{1,0:T(8,128)(2,1)}, u32[]{:S(2)}, u32[]{:S(2)}) collective-permute-start(bf16[128,1024]{1,0:T(8,128)(2,1)S(1)} %get-tuple-element.65), channel_id=1, source_target_pairs={{0,16},{1,18},{2,17},{3,19},{4,20},{5,22},{6,21},{7,23},{8,24},{9,... | collective-permute-start | bytes 786440 | tf_op jit(solution)/shard_map/ppermute | solution.py:27
  345.3 28.8 %collective-permute-start.70 = (bf16[128,3072]{1,0:T(8,128)(2,1)S(1)}, bf16[128,3072]{1,0:T(8,128)(2,1)S(1)}, u32[]{:S(2)}, u32[]{:S(2)}) collective-permute-start(bf16[128,3072]{1,0:T(8,128)(2,1)S(1)} %pad_maximum_fusion.6), channel_id=1, source_target_pairs={{0,1},{1,0},{2,3},{3,2},{4,5},{5,4},{6,7},{7,6},{8,9},{9,8},{10,11... | collective-permute-start | bytes 2359304 | tf_op jit(solution)/shard_map/ppermute | solution.py:27
  356.4 12.9 %collective-permute-start.62 = (bf16[128,1024]{1,0:T(8,128)(2,1)}, bf16[128,1024]{1,0:T(8,128)(2,1)S(1)}, u32[]{:S(2)}, u32[]{:S(2)}) collective-permute-start(bf16[128,1024]{1,0:T(8,128)(2,1)} %collective-permute-done.60.a0.c), channel_id=1, source_target_pairs={{0,12},{1,13},{2,14},{3,15},{4,0},{5,1},{6,2},{7,3},{8,4},{9,5},{1... | collective-permute-start | bytes 786440 | tf_op jit(solution)/shard_map/ppermute | solution.py:27
  369.3 34.4 %collective-permute-start.68 = (bf16[128,3072]{1,0:T(8,128)(2,1)}, bf16[128,3072]{1,0:T(8,128)(2,1)}, u32[]{:S(2)}, u32[]{:S(2)}) collective-permute-start(bf16[128,3072]{1,0:T(8,128)(2,1)} %pad_maximum_fusion.4), channel_id=1, source_target_pairs={{0,1},{1,0},{2,3},{3,2},{4,5},{5,4},{6,7},{7,6},{8,9},{9,8},{10,11... | collective-permute-start | bytes 2359304 | tf_op jit(solution)/shard_map/ppermute | solution.py:27
  369.7 37.4 %collective-permute-start.67 = (bf16[128,3072]{1,0:T(8,128)(2,1)}, bf16[128,3072]{1,0:T(8,128)(2,1)}, u32[]{:S(2)}, u32[]{:S(2)}) collective-permute-start(bf16[128,3072]{1,0:T(8,128)(2,1)} %pad_maximum_fusion.3), channel_id=1, source_target_pairs={{0,1},{1,0},{2,3},{3,2},{4,5},{5,4},{6,7},{7,6},{8,9},{9,8},{10,11... | collective-permute-start | bytes 2359304 | tf_op jit(solution)/shard_map/ppermute | solution.py:27
  370.7 41.8 %collective-permute-start.65 = (bf16[128,3072]{1,0:T(8,128)(2,1)}, bf16[128,3072]{1,0:T(8,128)(2,1)}, u32[]{:S(2)}, u32[]{:S(2)}) collective-permute-start(bf16[128,3072]{1,0:T(8,128)(2,1)} %pad_maximum_fusion.2), channel_id=1, source_target_pairs={{0,1},{1,0},{2,3},{3,2},{4,5},{5,4},{6,7},{7,6},{8,9},{9,8},{10,11... | collective-permute-start | bytes 2359304 | tf_op jit(solution)/shard_map/ppermute | solution.py:27
  375.0 35.4 %collective-permute-start.66 = (f32[128,1152]{1,0:T(8,128)S(1)}, f32[128,1152]{1,0:T(8,128)}, u32[]{:S(2)}, u32[]{:S(2)}) collective-permute-start(f32[128,1152]{1,0:T(8,128)S(1)} %project.21.a), channel_id=1, source_target_pairs={{0,1},{1,0},{2,3},{3,2},{4,5},{5,4},{6,7},{7,6},{8,9},{9,8},{10,11... | collective-permute-start | bytes 1769480 | tf_op jit(solution)/shard_map/ppermute | solution.py:27
  376.2 34.2 %collective-permute-start.64 = (bf16[128,1024]{1,0:T(8,128)(2,1)}, bf16[128,1024]{1,0:T(8,128)(2,1)}, u32[]{:S(2)}, u32[]{:S(2)}) collective-permute-start(bf16[128,1024]{1,0:T(8,128)(2,1)} %collective-permute-done.60.a0.c), channel_id=1, source_target_pairs={{0,1},{1,0},{2,3},{3,2},{4,5},{5,4},{6,7},{7,6},{8,9},{9,8},{10,11... | collective-permute-start | bytes 786440 | tf_op jit(solution)/shard_map/ppermute | solution.py:27
  420.9 18.1 %all-to-all-start.1 = ((bf16[16,4,8,512]{3,2,1,0:T(8,128)(2,1)}), bf16[16,4,8,512]{3,2,1,0:T(8,128)(2,1)S(1)}, u32[]{:S(2)}, u32[]{:S(2)}) async-start(bf16[16,4,8,512]{3,2,1,0:T(8,128)(2,1)} %copy_bitcast_fusion), calls=%async_computation.1 | async-start | bytes 1048576 | tf_op jit(solution)/shard_map/all_to_all | solution.py:259
  (200 other events, 4677.9 us)

commit v3 on v2

v3 whole, which is shorter than its diff:
```python
import jax
import jax.numpy as jnp
from jax import lax
from jax.experimental import pallas as pl
from jax.experimental.pallas import tpu as pltpu
from jax.sharding import PartitionSpec as P

epsilon = 1e-05
AXES = ("segment", "shard")
SEGMENTS, ROWS, COLUMNS, CORES = 8, 4, 2, 2
STEPS = (0, 1, 3, 2)
MIB = 1 << 20
PARTS = 1


def shard_of(row, column, core):
    return (row * COLUMNS + column) * CORES + core


def move(value, target):
    pairs = []
    for s in range(SEGMENTS):
        for row in range(ROWS):
            for column in range(COLUMNS):
                for core in range(CORES):
                    t, r, c, k = target(s, row, column, core)
                    pairs.append((s * 16 + shard_of(row, column, core), t % SEGMENTS * 16 + shard_of(r % ROWS, c, k)))
    return lax.ppermute(value, AXES, pairs)


def to_sibling(value):
    return move(value, lambda s, r, c, k: (s, r, c, 1 - k))


def up_rows(value, by):
    return move(value, lambda s, r, c, k: (s, r + by, c, k))


def next_segment(value):
    return move(value, lambda s, r, c, k: (s + 1, r, k, c))


def whole(shape):
    return pl.BlockSpec(shape, lambda *_: (0,) * len(shape))


def arrange_weights(place, weights, own):
    features, half = weights.shape
    block = features // (ROWS * COLUMNS)

    def kernel(place, source, out, sems):
        which = place[0] if own else 1 - place[0]
        copies = []
        for i, by in enumerate(STEPS):
            at = lax.rem(place[4] + ROWS - by, ROWS) * COLUMNS + which
            start = pl.multiple_of(at * block, block)
            copies.append(pltpu.make_async_copy(source.at[pl.ds(start, block)], out.at[pl.ds(i * block, block)], sems.at[i]))
        for c in copies:
            c.start()
        for c in copies:
            c.wait()

    return pl.pallas_call(
        kernel,
        in_specs=[pl.BlockSpec(memory_space=pltpu.SMEM), pl.BlockSpec(memory_space=pl.ANY)],
        out_specs=pl.BlockSpec(memory_space=pltpu.VMEM if own else pl.ANY),
        out_shape=(pltpu.VMEM if own else pltpu.HBM)((ROWS * block, half), weights.dtype),
        scratch_shapes=[pltpu.SemaphoreType.DMA((ROWS,))],
        compiler_params=pltpu.CompilerParams(vmem_limit_bytes=8 * MIB),
        cost_estimate=pl.CostEstimate(flops=0, bytes_accessed=8 * MIB, transcendentals=0),
        name="kept_rows" if own else "given_rows",
    )(place, weights)


def near(value):
    def kernel(source, out, sem):
        copy = pltpu.make_async_copy(source, out, sem)
        copy.start()
        copy.wait()

    return pl.pallas_call(
        kernel,
        in_specs=[pl.BlockSpec(memory_space=pl.ANY)],
        out_specs=pl.BlockSpec(memory_space=pltpu.VMEM),
        out_shape=pltpu.VMEM(value.shape, value.dtype),
        scratch_shapes=[pltpu.SemaphoreType.DMA],
        compiler_params=pltpu.CompilerParams(vmem_limit_bytes=8 * MIB),
        cost_estimate=pl.CostEstimate(flops=0, bytes_accessed=8 * MIB, transcendentals=0),
        name="near",
    )(value)


def project(blocks, kept, swapped, after):
    tokens, block = blocks[0].shape
    half = kept.shape[1]

    def kernel(a0, a1, a2, a3, kept, swapped, *refs):
        out = refs[-1]
        step = pl.program_id(0)
        for which, value in enumerate((a0, a1, a2, a3)):

            @pl.when(step == which)
            def _():
                x = value[...]
                floats = x.astype(jnp.float32)
                squares = jnp.sum(floats * floats, axis=1, keepdims=True)
                squares = jnp.broadcast_to(squares, (tokens, 128))
                mine = jnp.dot(x, kept[...], preferred_element_type=jnp.float32)
                others = jnp.dot(x, swapped[...], preferred_element_type=jnp.float32)
                if which == 0:
                    out[:, :half] = mine
                    out[:, half : 2 * half] = others
                    out[:, 2 * half :] = squares
                else:
                    out[:, :half] += mine
                    out[:, half : 2 * half] += others
                    out[:, 2 * half :] += squares

    return pl.pallas_call(
        kernel,
        grid=(len(blocks),),
        in_specs=[whole((tokens, block))] * 4
        + [pl.BlockSpec((block, half), lambda i: (i, 0))] * 2
        + [pl.BlockSpec(memory_space=pl.ANY)] * len(after),
        out_specs=whole((tokens, 2 * half + 128)),
        out_shape=jax.ShapeDtypeStruct((tokens, 2 * half + 128), jnp.float32),
        compiler_params=pltpu.CompilerParams(vmem_limit_bytes=16 * MIB),
        cost_estimate=pl.CostEstimate(flops=2 * tokens * 8 * half * 2 * half, bytes_accessed=9 * MIB, transcendentals=0),
        name="project",
    )(*blocks, kept, swapped, *after)


def combine(place, own, came, held, other_held, fresh, features):
    tokens, block = held.shape

    def kernel(place, own, came, held, other_held, fresh, block_out, scale_out):
        half = block // 2
        core, column, segment = place[0], place[1], place[2]
        total = own[:, block:] + came[:, block:]
        scale = lax.rsqrt(total * (1.0 / features) + epsilon)
        scale_out[...] = scale
        factor = scale[:, :1]
        mine = (own[:, :half] + came[:, half:block]) * factor
        others = (own[:, half:block] + came[:, :half]) * factor
        residual = jnp.where(core == column, held[...], other_held[...]).astype(jnp.float32)
        low = (residual[:, :half] + jnp.where(core == 0, mine, others)).astype(jnp.bfloat16)
        high = (residual[:, half:] + jnp.where(core == 0, others, mine)).astype(jnp.bfloat16)
        if fresh is not None:
            last = segment == SEGMENTS - 1
            low = jnp.where(last, fresh[:, :half], low)
            high = jnp.where(last, fresh[:, half:], high)
        block_out[:, :half] = low
        block_out[:, half:] = high

    operands = [own, came, held, other_held]
    if fresh is not None:
        operands.append(fresh)
        run = kernel
    else:
        run = lambda p, a, b, c, d, *outs: kernel(p, a, b, c, d, None, *outs)
    return pl.pallas_call(
        run,
        in_specs=[pl.BlockSpec(memory_space=pltpu.SMEM)] + [pl.BlockSpec(memory_space=pltpu.VMEM)] * len(operands),
        out_specs=[pl.BlockSpec(memory_space=pltpu.VMEM)] * 2,
        out_shape=[
            jax.ShapeDtypeStruct((tokens, block), jnp.bfloat16),
            jax.ShapeDtypeStruct((tokens, 128), jnp.float32),
        ],
        compiler_params=pltpu.CompilerParams(vmem_limit_bytes=8 * MIB),
        cost_estimate=pl.CostEstimate(flops=8 * tokens * block, bytes_accessed=2 * MIB, transcendentals=0),
        name="combine",
    )(place, *operands)


def record(table, blocks, others, rest, scale, result):
    tokens, block = blocks[0].shape

    def kernel(table, a0, a1, a2, a3, b0, rest, scale, result, out, act, done):
        step = pl.program_id(0)
        act[...] = result[...]
        factor = scale[:, :1]
        done[...] = jnp.zeros_like(done)
        for which, value in enumerate((a0, a1, a2, a3, b0)):

            @pl.when(step == which)
            def _():
                out[...] = (value[...].astype(jnp.float32) * factor).astype(jnp.bfloat16)

        for which in range(3):

            @pl.when(step == 5 + which)
            def _():
                piece = rest[:, which * block : (which + 1) * block]
                out[...] = (piece.astype(jnp.float32) * factor).astype(jnp.bfloat16)

    return pl.pallas_call(
        kernel,
        grid_spec=pltpu.PrefetchScalarGridSpec(
            num_scalar_prefetch=1,
            grid=(8,),
            in_specs=[whole((tokens, block))] * 5
            + [whole(rest.shape), whole(scale.shape), pl.BlockSpec((tokens, block // 2), lambda i, t: (0, t[8]))],
            out_specs=[
                pl.BlockSpec((tokens, block), lambda i, t: (0, t[i])),
                whole((tokens, block // 2)),
                whole((8, 128)),
            ],
        ),
        out_shape=[
            pltpu.HBM((tokens, 8 * block), jnp.bfloat16),
            pltpu.HBM((tokens, block // 2), jnp.bfloat16),
            jax.ShapeDtypeStruct((8, 128), jnp.float32),
        ],
        compiler_params=pltpu.CompilerParams(vmem_limit_bytes=8 * MIB),
        cost_estimate=pl.CostEstimate(flops=16 * tokens * block, bytes_accessed=5 * MIB, transcendentals=0),
        name="record",
    )(table, *blocks, others, rest, scale, result)


def gram_of(place, pieces, micros, width):
    tokens, features = pieces[0][0].shape
    parts = len(pieces[0])
    pieces = [pltpu.with_memory_space_constraint(p, pltpu.HBM) for tick in pieces for p in tick]
    groups = micros * parts
    count = groups * tokens
    step = 1024
    steps = features // step

    def kernel(place, *refs):
        sources, (out, every, own, turned, arrived, own_arrived) = refs[: len(pieces)], refs[len(pieces) :]
        segment, device = place[2], place[3]
        now = pl.program_id(0)
        own_start = pl.multiple_of(device * width, width)

        def copies(s, columns):
            for g in range(groups):
                source = sources[s * parts + g]
                rows = pl.ds(g * tokens, tokens)
                if columns is None:
                    yield pltpu.make_async_copy(source.at[:, pl.ds(own_start, width)], own.at[rows], own_arrived.at[g])
                else:
                    at = pl.ds(columns * step, step)
                    yield pltpu.make_async_copy(source.at[:, at], every.at[columns, rows], arrived.at[columns, g])

        @pl.when(now == 0)
        def _():
            for s in range(SEGMENTS):

                @pl.when(segment == s)
                def _():
                    for columns in [None, *range(steps)]:
                        for c in copies(s, columns):
                            c.start()

            for c in copies(0, None):
                c.wait()
            turned[...] = own[...].T

        for columns in range(steps):

            @pl.when(now == columns)
            def _():
                for c in copies(0, columns):
                    c.wait()
                out[...] = jnp.dot(turned[...], every[columns], preferred_element_type=jnp.float32) * (1.0 / count)

    return pl.pallas_call(
        kernel,
        grid=(steps,),
        in_specs=[pl.BlockSpec(memory_space=pltpu.SMEM)] + [pl.BlockSpec(memory_space=pltpu.HBM)] * len(pieces),
        out_specs=pl.BlockSpec((width, step), lambda i: (0, i)),
        out_shape=jax.ShapeDtypeStruct((width, features), jnp.float32),
        scratch_shapes=[
            pltpu.VMEM((steps, count, step), jnp.bfloat16),
            pltpu.VMEM((count, width), jnp.bfloat16),
            pltpu.VMEM((width, count), jnp.bfloat16),
            pltpu.SemaphoreType.DMA((steps, groups)),
            pltpu.SemaphoreType.DMA((groups,)),
        ],
        compiler_params=pltpu.CompilerParams(vmem_limit_bytes=24 * MIB),
        cost_estimate=pl.CostEstimate(flops=2 * count * width * features, bytes_accessed=26 * MIB, transcendentals=0),
        name="gram",
    )(place, *pieces)


def body(tokens_in, weights):
    micros, rows, features = tokens_in.shape
    shards = 16
    batch = rows * shards
    block = features // 8
    half = block // 2
    device = lax.axis_index("shard")
    segment = lax.axis_index("segment")
    core = device % 2
    column = device // 2 % 2
    row = device // 4
    place = jnp.stack([core, column, segment, device, row]).astype(jnp.int32)

    swapped = near(to_sibling(arrange_weights(place, weights[0], False)))
    kept = arrange_weights(place, weights[0], True)

    split = tokens_in[0].reshape(rows, ROWS, CORES, block).transpose(2, 0, 1, 3).reshape(1, CORES, rows, ROWS * block)
    split = jnp.broadcast_to(split, (ROWS * COLUMNS, CORES, rows, ROWS * block)).reshape(shards, rows, ROWS * block)
    later = tokens_in[1:].reshape(micros - 1, rows, shards, half).transpose(2, 1, 0, 3).reshape(shards, rows, -1)
    arrived = lax.all_to_all(jnp.concatenate([split, later], axis=2), "shard", 0, 0).reshape(batch, -1)
    waiting = arrived[:, ROWS * block :]
    paired = to_sibling(waiting)
    from_rows = [(row + ROWS - by) % ROWS for by in STEPS]
    feature_table = [r * COLUMNS + k for k in (core, 1 - core) for r in from_rows]
    feature_table = jnp.stack(feature_table + [core]).astype(jnp.int32)
    first_blocks = [lax.dynamic_slice(arrived, (0, r * block), (batch, block)) for r in from_rows]

    def fresh_of(micro, lo, hi):
        a, b = (v[lo:hi, (micro - 1) * half : micro * half] for v in (waiting, paired))
        return jnp.where(core == 0, jnp.concatenate([a, b], 1), jnp.concatenate([b, a], 1))

    size = batch // PARTS
    chip_blocks = [None] * PARTS
    after = [()] * PARTS
    inputs, acts = [], []
    for tick in range(micros + SEGMENTS - 1):
        inputs.append([])
        acts.append([])
        for part in range(PARTS):
            lo, hi = part * size, (part + 1) * size
            if tick == 0:
                blocks = [b[lo:hi] for b in first_blocks]
                held = blocks[0]
            else:
                held = next_segment(chip_blocks[part])
                blocks = [held] + [up_rows(held, by) for by in STEPS[1:]]
            other_held = to_sibling(held)
            own = project(blocks, kept, swapped, after[part])
            came = to_sibling(own)
            fresh = fresh_of(tick + 1, lo, hi) if tick + 1 < micros else None
            chip_blocks[part], scale = combine(place, own, came, held, other_held, fresh, features)
            rest = to_sibling(jnp.concatenate(blocks[1:], axis=1))
            normed, act, done = record(feature_table, blocks, other_held, rest, scale, chip_blocks[part])
            inputs[-1].append(normed)
            acts[-1].append(act)
            after[part] = (done,)

    acts = jnp.stack([jnp.concatenate(a, axis=0) for a in acts])
    acts = lax.dynamic_slice(acts, (segment, 0, 0), (micros, batch, half))
    outgoing = acts.reshape(micros, shards, rows, half).transpose(1, 0, 2, 3)
    arrived = lax.all_to_all(outgoing, "shard", 0, 0)
    outputs = arrived.transpose(1, 2, 0, 3).reshape(micros, rows, features)
    return (outputs[None], gram_of(place, inputs, micros, half)[None])


def solution(mesh):
    in_specs = (P(None, "shard", None), P("segment", None, "shard"))
    out_specs = (P("segment", None, "shard", None), P("segment", "shard", None))
    return jax.shard_map(body, mesh=mesh, in_specs=in_specs, out_specs=out_specs, check_vma=False)
```

time: 450 us -> 416 us (0.924)
  waiting for transfers between devices: 251 us -> 220 us
  Pallas kernels: 67 us -> 96.1 us
  blocking collectives: 21.3 us -> 0 us
  local copies, waits for them, and re-layouts: 34.9 us -> 27.3 us
    ppermute x77 -> x75, waiting for transfers between devices: 251 us -> 206 us  [move(): return lax.ppermute(value, AXES, pairs)]
    pallas_call x11, Pallas kernels: 26.4 us -> 47.9 us  [record(): pl.pallas_call(kernel, grid_spec=pltpu.PrefetchScalarGridSpec(num_scalar_...]
    all_to_all x1 -> x0, blocking collectives: 21.3 us -> none  [body(): arrived = lax.all_to_all(outgoing, 'shard', 0, 0)]
    all_to_all x0 -> x1, waiting for transfers between devices: none -> 13.8 us  [body(): lax.all_to_all(jnp.concatenate([split, later], axis=2), 'shard', 0, 0)]
    pallas_call x12 -> x15, Pallas kernels: 31.2 us -> 40.3 us  [the longest x11 20.7 us: project(): pl.pallas_call(kernel, grid=(len(blocks),), in_specs=[whole((tokens, bloc...]
    all_to_all x0 -> x1, starting transfers between devices: none -> 6.26 us  [body(): lax.all_to_all(jnp.concatenate([split, later], axis=2), 'shard', 0, 0)]
    ppermute x77 -> x75, starting transfers between devices: 54 us -> 49.1 us  [move(): return lax.ppermute(value, AXES, pairs)]
    unnamed x308 -> x56, local copies, waits for them, and re-layouts: 22.9 us -> 21 us
  transfers between devices with their start and end apart: 78 -> 77, of which waited for: 52 -> 44; matrix products, arithmetic and copies ran while one was open for 2% -> 2% of each run, Pallas kernels for 9% -> 18%
where the time goes in v3:
time: 416 us; the launch traced here: 408 us
  waiting for transfers between devices  220 us (53%)
  Pallas kernels  96.1 us (23%)
  starting transfers between devices  59.1 us (14%)
  local copies, waits for them, and re-layouts  27.3 us (7%)
    ppermute x75, waiting for transfers between devices, move(): return lax.ppermute(value, AXES, pairs)  206 us
    ppermute x75, starting transfers between devices, move(): return lax.ppermute(value, AXES, pairs)  49.1 us
    pallas_call x11, Pallas kernels, record(): pl.pallas_call(kernel, grid_spec=pltpu.PrefetchScalarGridSpec(num_scalar_...  47.9 us
    unnamed x56, local copies, waits for them, and re-layouts  21 us
    pallas_call x11, Pallas kernels, project(): pl.pallas_call(kernel, grid=(len(blocks),), in_specs=[whole((tokens, bloc...  20.7 us
    all_to_all x1, waiting for transfers between devices, body(): lax.all_to_all(jnp.concatenate([split, later], axis=2), 'shard', 0, 0)  13.8 us
    pallas_call x1, Pallas kernels, gram_of(): pl.pallas_call(kernel, grid=(steps,), in_specs=[pl.BlockSpec(memory_space...  13.7 us
  transfers between devices with their start and end apart: 77, of which 44 were waited for; matrix products, arithmetic and copies ran while one was open for 2% of the time, Pallas kernels for 18%

profile of v3, /device:TPU:1, one launch (start us, length us, event | category | flops | bytes accessed | tf_op | source)
XLA Modules:
  0.0 407.7 jit_solution(7165798120369249621)
XLA Ops:
  9.8 6.3 %all-to-all-start = ((bf16[16,8,5632]{2,1,0:T(8,128)(2,1)}), bf16[16,8,5632]{2,1,0:T(8,128)(2,1)S(1)}, u32[]{:S(2)}, u32[]{:S(2)}) async-start(bf16[16,8,5632]{2,1,0:T(8,128)(2,1)} %pad_maximum_fusion), calls=%async_computation | async-start | bytes 2883584 | tf_op jit(solution)/shard_map/all_to_all | solution.py:305
  22.4 13.8 %all-to-all-done = bf16[16,8,5632]{2,1,0:T(8,128)(2,1)S(1)} async-done(((bf16[16,8,5632]{2,1,0:T(8,128)(2,1)}), bf16[16,8,5632]{2,1,0:T(8,128)(2,1)S(1)}, u32[]{:S(2)}, u32[]{:S(2)}) %all-to-all-start) | async-done | bytes 1441824 | tf_op jit(solution)/shard_map/all_to_all | solution.py:305
  50.6 10.3 %collective-permute-done.5.a0.held = bf16[128,1024]{1,0:T(8,128)(2,1)S(1)} collective-permute-done((bf16[128,1024]{1,0:T(8,128)(2,1)S(1)}, bf16[128,1024]{1,0:T(8,128)(2,1)S(1)}, u32[]{:S(2)}, u32[]{:S(2)}) %collective-permute-start.5) | collective-permute-done | bytes 262176 | tf_op jit(solution)/shard_map/ppermute | solution.py:28
  63.7 4.4 %record.11 = (bf16[128,8192]{1,0:T(8,128)(2,1)}, bf16[128,512]{1,0:T(8,128)(2,1)}, f32[8,128]{1,0:T(8,128)S(1)}) custom-call(s32[9]{0:T(128)S(1)} %stack.91.table, bf16[128,1024]{1,0:T(8,128)(2,1)S(1)} %get-tuple-element.116.a0.held, bf16[128,1024]{1,0:T(8,128)(2,1)S(1)} %get-tuple-element.115.a1, bf16[128,1024]{1,0:T(8,128)(2,1)S(1)} %get-tuple-element.114.a2, ...), custom_call_target="tpu_custom_call" | custom-call | flops 2097152 | bytes 5242880 | tf_op jit(solution)/shard_map/record/pallas_call | solution.py:196
  68.1 6.9 %collective-permute-done.6.a1 = bf16[128,1024]{1,0:T(8,128)(2,1)S(1)} collective-permute-done((bf16[128,1024]{1,0:T(8,128)(2,1)S(1)}, bf16[128,1024]{1,0:T(8,128)(2,1)S(1)}, u32[]{:S(2)}, u32[]{:S(2)}) %collective-permute-start.6) | collective-permute-done | bytes 262176 | tf_op jit(solution)/shard_map/ppermute | solution.py:28
  85.7 11.9 %collective-permute-done.12.a0.held = bf16[128,1024]{1,0:T(8,128)(2,1)S(1)} collective-permute-done((bf16[128,1024]{1,0:T(8,128)(2,1)S(1)}, bf16[128,1024]{1,0:T(8,128)(2,1)S(1)}, u32[]{:S(2)}, u32[]{:S(2)}) %collective-permute-start.12) | collective-permute-done | bytes 262176 | tf_op jit(solution)/shard_map/ppermute | solution.py:28
  101.9 4.4 %record.12 = (bf16[128,8192]{1,0:T(8,128)(2,1)}, bf16[128,512]{1,0:T(8,128)(2,1)}, f32[8,128]{1,0:T(8,128)S(1)}) custom-call(s32[9]{0:T(128)S(1)} %stack.91.table, bf16[128,1024]{1,0:T(8,128)(2,1)S(1)} %collective-permute-done.5.a0.held, bf16[128,1024]{1,0:T(8,128)(2,1)S(1)} %collective-permute-done.6.a1, bf16[128,1024]{1,0:T(8,128)(2,1)S(1)} %collective-permute-done.7.a2, ...), custom_call_target="tpu_custom_call" | custom-call | flops 2097152 | bytes 5242880 | tf_op jit(solution)/shard_map/record/pallas_call | solution.py:196
  106.3 4.9 %collective-permute-done.14.a2 = bf16[128,1024]{1,0:T(8,128)(2,1)S(1)} collective-permute-done((bf16[128,1024]{1,0:T(8,128)(2,1)S(1)}, bf16[128,1024]{1,0:T(8,128)(2,1)S(1)}, u32[]{:S(2)}, u32[]{:S(2)}) %collective-permute-start.14) | collective-permute-done | bytes 262176 | tf_op jit(solution)/shard_map/ppermute | solution.py:28
  119.1 11.9 %collective-permute-done.19.a0.c = bf16[128,1024]{1,0:T(8,128)(2,1)S(1)} collective-permute-done((bf16[128,1024]{1,0:T(8,128)(2,1)S(1)}, bf16[128,1024]{1,0:T(8,128)(2,1)S(1)}, u32[]{:S(2)}, u32[]{:S(2)}) %collective-permute-start.19) | collective-permute-done | bytes 262176 | tf_op jit(solution)/shard_map/ppermute | solution.py:28
  134.0 4.4 %record.13 = (bf16[128,8192]{1,0:T(8,128)(2,1)}, bf16[128,512]{1,0:T(8,128)(2,1)}, f32[8,128]{1,0:T(8,128)S(1)}) custom-call(s32[9]{0:T(128)S(1)} %stack.91.table, bf16[128,1024]{1,0:T(8,128)(2,1)S(1)} %collective-permute-done.12.a0.held, bf16[128,1024]{1,0:T(8,128)(2,1)S(1)} %collective-permute-done.13.a1, ...), custom_call_target="tpu_custom_call" | custom-call | flops 2097152 | bytes 5242880 | tf_op jit(solution)/shard_map/record/pallas_call | solution.py:196
  150.9 11.9 %collective-permute-done.26.a0.c = bf16[128,1024]{1,0:T(8,128)(2,1)S(1)} collective-permute-done((bf16[128,1024]{1,0:T(8,128)(2,1)S(1)}, bf16[128,1024]{1,0:T(8,128)(2,1)S(1)}, u32[]{:S(2)}, u32[]{:S(2)}) %collective-permute-start.26) | collective-permute-done | bytes 262176 | tf_op jit(solution)/shard_map/ppermute | solution.py:28
  167.0 4.4 %record.14 = (bf16[128,8192]{1,0:T(8,128)(2,1)}, bf16[128,512]{1,0:T(8,128)(2,1)}, f32[8,128]{1,0:T(8,128)S(1)}) custom-call(s32[9]{0:T(128)S(1)} %stack.91.table, bf16[128,1024]{1,0:T(8,128)(2,1)S(1)} %collective-permute-done.19.a0.c, bf16[128,1024]{1,0:T(8,128)(2,1)S(1)} %collective-permute-done.20.a1, bf16[128,1024]{1,0:T(8,128)(2,1)S(1)} %collective-permute-done.21.a2, ...), custom_call_target="tpu_custom_call" | custom-call | flops 2097152 | bytes 5242880 | tf_op jit(solution)/shard_map/record/pallas_call | solution.py:196
  171.4 4.9 %collective-permute-done.28.a2 = bf16[128,1024]{1,0:T(8,128)(2,1)S(1)} collective-permute-done((bf16[128,1024]{1,0:T(8,128)(2,1)S(1)}, bf16[128,1024]{1,0:T(8,128)(2,1)S(1)}, u32[]{:S(2)}, u32[]{:S(2)}) %collective-permute-start.28) | collective-permute-done | bytes 262176 | tf_op jit(solution)/shard_map/ppermute | solution.py:28
  184.6 11.9 %collective-permute-done.33.a0.c = bf16[128,1024]{1,0:T(8,128)(2,1)S(1)} collective-permute-done((bf16[128,1024]{1,0:T(8,128)(2,1)S(1)}, bf16[128,1024]{1,0:T(8,128)(2,1)S(1)}, u32[]{:S(2)}, u32[]{:S(2)}) %collective-permute-start.33) | collective-permute-done | bytes 262176 | tf_op jit(solution)/shard_map/ppermute | solution.py:28
  199.5 4.4 %record.15 = (bf16[128,8192]{1,0:T(8,128)(2,1)}, bf16[128,512]{1,0:T(8,128)(2,1)}, f32[8,128]{1,0:T(8,128)S(1)}) custom-call(s32[9]{0:T(128)S(1)} %stack.91.table, bf16[128,1024]{1,0:T(8,128)(2,1)S(1)} %collective-permute-done.26.a0.c, bf16[128,1024]{1,0:T(8,128)(2,1)S(1)} %collective-permute-done.27.a1, bf16[128,1024]{1,0:T(8,128)(2,1)S(1)} %collective-permute-done.28.a2, ...), custom_call_target="tpu_custom_call" | custom-call | flops 2097152 | bytes 5242880 | tf_op jit(solution)/shard_map/record/pallas_call | solution.py:196
  206.1 3.9 collective-permute-done.35.a2
  216.5 11.9 %collective-permute-done.40.a0.c = bf16[128,1024]{1,0:T(8,128)(2,1)S(1)} collective-permute-done((bf16[128,1024]{1,0:T(8,128)(2,1)S(1)}, bf16[128,1024]{1,0:T(8,128)(2,1)S(1)}, u32[]{:S(2)}, u32[]{:S(2)}) %collective-permute-start.40) | collective-permute-done | bytes 262176 | tf_op jit(solution)/shard_map/ppermute | solution.py:28
  232.5 4.3 %record.16 = (bf16[128,8192]{1,0:T(8,128)(2,1)}, bf16[128,512]{1,0:T(8,128)(2,1)}, f32[8,128]{1,0:T(8,128)S(1)}) custom-call(s32[9]{0:T(128)S(1)} %stack.91.table, bf16[128,1024]{1,0:T(8,128)(2,1)S(1)} %collective-permute-done.33.a0.c, bf16[128,1024]{1,0:T(8,128)(2,1)S(1)} %collective-permute-done.34.a1, bf16[128,1024]{1,0:T(8,128)(2,1)S(1)} %collective-permute-done.35.a2, ...), custom_call_target="tpu_custom_call" | custom-call | flops 2097152 | bytes 5242880 | tf_op jit(solution)/shard_map/record/pallas_call | solution.py:196
  236.8 5.0 %collective-permute-done.42.a2 = bf16[128,1024]{1,0:T(8,128)(2,1)S(1)} collective-permute-done((bf16[128,1024]{1,0:T(8,128)(2,1)S(1)}, bf16[128,1024]{1,0:T(8,128)(2,1)S(1)}, u32[]{:S(2)}, u32[]{:S(2)}) %collective-permute-start.42) | collective-permute-done | bytes 262176 | tf_op jit(solution)/shard_map/ppermute | solution.py:28
  249.7 11.9 %collective-permute-done.47.a0.c = bf16[128,1024]{1,0:T(8,128)(2,1)S(1)} collective-permute-done((bf16[128,1024]{1,0:T(8,128)(2,1)S(1)}, bf16[128,1024]{1,0:T(8,128)(2,1)S(1)}, u32[]{:S(2)}, u32[]{:S(2)}) %collective-permute-start.47) | collective-permute-done | bytes 262176 | tf_op jit(solution)/shard_map/ppermute | solution.py:28
  264.6 4.4 %record.17 = (bf16[128,8192]{1,0:T(8,128)(2,1)}, bf16[128,512]{1,0:T(8,128)(2,1)}, f32[8,128]{1,0:T(8,128)S(1)}) custom-call(s32[9]{0:T(128)S(1)} %stack.91.table, bf16[128,1024]{1,0:T(8,128)(2,1)S(1)} %collective-permute-done.40.a0.c, bf16[128,1024]{1,0:T(8,128)(2,1)S(1)} %collective-permute-done.41.a1, bf16[128,1024]{1,0:T(8,128)(2,1)S(1)} %collective-permute-done.42.a2, ...), custom_call_target="tpu_custom_call" | custom-call | flops 2097152 | bytes 5242880 | tf_op jit(solution)/shard_map/record/pallas_call | solution.py:196
  271.2 3.9 collective-permute-done.49.a2
  281.5 11.9 %collective-permute-done.54.a0.c = bf16[128,1024]{1,0:T(8,128)(2,1)S(1)} collective-permute-done((bf16[128,1024]{1,0:T(8,128)(2,1)S(1)}, bf16[128,1024]{1,0:T(8,128)(2,1)S(1)}, u32[]{:S(2)}, u32[]{:S(2)}) %collective-permute-start.54) | collective-permute-done | bytes 262176 | tf_op jit(solution)/shard_map/ppermute | solution.py:28
  297.6 4.3 %record.18 = (bf16[128,8192]{1,0:T(8,128)(2,1)}, bf16[128,512]{1,0:T(8,128)(2,1)}, f32[8,128]{1,0:T(8,128)S(1)}) custom-call(s32[9]{0:T(128)S(1)} %stack.91.table, bf16[128,1024]{1,0:T(8,128)(2,1)S(1)} %collective-permute-done.47.a0.c, bf16[128,1024]{1,0:T(8,128)(2,1)S(1)} %collective-permute-done.48.a1, bf16[128,1024]{1,0:T(8,128)(2,1)S(1)} %collective-permute-done.49.a2, ...), custom_call_target="tpu_custom_call" | custom-call | flops 2097152 | bytes 5242880 | tf_op jit(solution)/shard_map/record/pallas_call | solution.py:196
  301.9 5.0 %collective-permute-done.56.a2 = bf16[128,1024]{1,0:T(8,128)(2,1)S(1)} collective-permute-done((bf16[128,1024]{1,0:T(8,128)(2,1)S(1)}, bf16[128,1024]{1,0:T(8,128)(2,1)S(1)}, u32[]{:S(2)}, u32[]{:S(2)}) %collective-permute-start.56) | collective-permute-done | bytes 262176 | tf_op jit(solution)/shard_map/ppermute | solution.py:28
  314.9 11.9 %collective-permute-done.61.a0.c = bf16[128,1024]{1,0:T(8,128)(2,1)S(1)} collective-permute-done((bf16[128,1024]{1,0:T(8,128)(2,1)S(1)}, bf16[128,1024]{1,0:T(8,128)(2,1)S(1)}, u32[]{:S(2)}, u32[]{:S(2)}) %collective-permute-start.61) | collective-permute-done | bytes 262176 | tf_op jit(solution)/shard_map/ppermute | solution.py:28
  330.7 4.4 %record.19 = (bf16[128,8192]{1,0:T(8,128)(2,1)}, bf16[128,512]{1,0:T(8,128)(2,1)}, f32[8,128]{1,0:T(8,128)S(1)}) custom-call(s32[9]{0:T(128)S(1)} %stack.91.table, bf16[128,1024]{1,0:T(8,128)(2,1)S(1)} %collective-permute-done.54.a0.c, bf16[128,1024]{1,0:T(8,128)(2,1)S(1)} %collective-permute-done.55.a1, bf16[128,1024]{1,0:T(8,128)(2,1)S(1)} %collective-permute-done.56.a2, ...), custom_call_target="tpu_custom_call" | custom-call | flops 2097152 | bytes 5242880 | tf_op jit(solution)/shard_map/record/pallas_call | solution.py:196
  350.0 11.9 %collective-permute-done.68.a0.c = bf16[128,1024]{1,0:T(8,128)(2,1)S(1)} collective-permute-done((bf16[128,1024]{1,0:T(8,128)(2,1)S(1)}, bf16[128,1024]{1,0:T(8,128)(2,1)S(1)}, u32[]{:S(2)}, u32[]{:S(2)}) %collective-permute-start.68) | collective-permute-done | bytes 262176 | tf_op jit(solution)/shard_map/ppermute | solution.py:28
  366.1 4.3 %record.20 = (bf16[128,8192]{1,0:T(8,128)(2,1)}, bf16[128,512]{1,0:T(8,128)(2,1)}, f32[8,128]{1,0:T(8,128)S(1)}) custom-call(s32[9]{0:T(128)S(1)} %stack.91.table, bf16[128,1024]{1,0:T(8,128)(2,1)S(1)} %collective-permute-done.61.a0.c, bf16[128,1024]{1,0:T(8,128)(2,1)S(1)} %collective-permute-done.62.a1, bf16[128,1024]{1,0:T(8,128)(2,1)S(1)} %collective-permute-done.63.a2, ...), custom_call_target="tpu_custom_call" | custom-call | flops 2097152 | bytes 5242880 | tf_op jit(solution)/shard_map/record/pallas_call | solution.py:196
  370.4 4.9 %collective-permute-done.70.a2 = bf16[128,1024]{1,0:T(8,128)(2,1)S(1)} collective-permute-done((bf16[128,1024]{1,0:T(8,128)(2,1)S(1)}, bf16[128,1024]{1,0:T(8,128)(2,1)S(1)}, u32[]{:S(2)}, u32[]{:S(2)}) %collective-permute-start.70) | collective-permute-done | bytes 262176 | tf_op jit(solution)/shard_map/ppermute | solution.py:28
  382.5 4.3 %record.21 = (bf16[128,8192]{1,0:T(8,128)(2,1)}, bf16[128,512]{1,0:T(8,128)(2,1)}, f32[8,128]{1,0:T(8,128)}) custom-call(s32[9]{0:T(128)S(1)} %stack.91.table, bf16[128,1024]{1,0:T(8,128)(2,1)S(1)} %collective-permute-done.68.a0.c, bf16[128,1024]{1,0:T(8,128)(2,1)S(1)} %collective-permute-done.69.a1, bf16[128,1024]{1,0:T(8,128)(2,1)S(1)} %collective-permute-done.70.a2, ...), custom_call_target="tpu_custom_call" | custom-call | flops 2097152 | bytes 5242880 | tf_op jit(solution)/shard_map/record/pallas_call | solution.py:196
  392.4 13.7 %gram.1 = f32[512,8192]{1,0:T(8,128)} custom-call(s32[5]{0:T(128)S(1)} %stack.96.place.p, bf16[128,8192]{1,0:T(8,128)(2,1)} %get-tuple-element.99.refs_0_, bf16[128,8192]{1,0:T(8,128)(2,1)} %get-tuple-element.100.refs_1_, bf16[128,8192]{1,0:T(8,128)(2,1)} %get-tuple-element.101.refs_2_, bf16[128,8192]{1,0:T(8,128)(2,1)} %get-tuple-element.102.refs_3_, ...), custom_call_target="tpu_custom_call" | custom-call | flops 4294967296 | bytes 27262976 | tf_op jit(solution)/shard_map/gram/pallas_call | solution.py:267
  (249 shorter events, 167.2 us)
Async XLA Ops:
  6.8 32.9 %collective-permute-start.2 = (bf16[4096,512]{1,0:T(8,128)(2,1)}, bf16[4096,512]{1,0:T(8,128)(2,1)}, u32[]{:S(2)}, u32[]{:S(2)}) collective-permute-start(bf16[4096,512]{1,0:T(8,128)(2,1)} %given_rows.1), channel_id=1, source_target_pairs={{0,1},{1,0},{2,3},{3,2},{4,5},{5,4},{6,7},{7,6},{8,9},{9,8},{10,11... | collective-permute-start | bytes 12582920 | tf_op jit(solution)/shard_map/ppermute | solution.py:28
  9.8 26.4 %all-to-all-start = ((bf16[16,8,5632]{2,1,0:T(8,128)(2,1)}), bf16[16,8,5632]{2,1,0:T(8,128)(2,1)S(1)}, u32[]{:S(2)}, u32[]{:S(2)}) async-start(bf16[16,8,5632]{2,1,0:T(8,128)(2,1)} %pad_maximum_fusion), calls=%async_computation | async-start | bytes 2883584 | tf_op jit(solution)/shard_map/all_to_all | solution.py:305
  39.1 24.6 %collective-permute-start.1 = (bf16[128,3072]{1,0:T(8,128)(2,1)}, bf16[128,3072]{1,0:T(8,128)(2,1)S(1)}, u32[]{:S(2)}, u32[]{:S(2)}) collective-permute-start(bf16[128,3072]{1,0:T(8,128)(2,1)} %pad_maximum_fusion.1), channel_id=1, source_target_pairs={{0,1},{1,0},{2,3},{3,2},{4,5},{5,4},{6,7},{7,6},{8,9},{9,8},{10,11... | collective-permute-start | bytes 2359304 | tf_op jit(solution)/shard_map/ppermute | solution.py:28
  48.5 12.5 %collective-permute-start.5 = (bf16[128,1024]{1,0:T(8,128)(2,1)S(1)}, bf16[128,1024]{1,0:T(8,128)(2,1)S(1)}, u32[]{:S(2)}, u32[]{:S(2)}) collective-permute-start(bf16[128,1024]{1,0:T(8,128)(2,1)S(1)} %get-tuple-element.57.result), channel_id=1, source_target_pairs={{0,16},{1,18},{2,17},{3,19},{4,20},{5,22},{6,21},{7,23},{8,24},{9,... | collective-permute-start | bytes 786440 | tf_op jit(solution)/shard_map/ppermute | solution.py:28
  60.9 14.1 %collective-permute-start.6 = (bf16[128,1024]{1,0:T(8,128)(2,1)S(1)}, bf16[128,1024]{1,0:T(8,128)(2,1)S(1)}, u32[]{:S(2)}, u32[]{:S(2)}) collective-permute-start(bf16[128,1024]{1,0:T(8,128)(2,1)S(1)} %collective-permute-done.5.a0.held), channel_id=1, source_target_pairs={{0,4},{1,5},{2,6},{3,7},{4,8},{5,9},{6,10},{7,11},{8,12},{9,13},{1... | collective-permute-start | bytes 786440 | tf_op jit(solution)/shard_map/ppermute | solution.py:28
  60.9 14.1 %collective-permute-start.7 = (bf16[128,1024]{1,0:T(8,128)(2,1)S(1)}, bf16[128,1024]{1,0:T(8,128)(2,1)S(1)}, u32[]{:S(2)}, u32[]{:S(2)}) collective-permute-start(bf16[128,1024]{1,0:T(8,128)(2,1)S(1)} %collective-permute-done.5.a0.held), channel_id=1, source_target_pairs={{0,12},{1,13},{2,14},{3,15},{4,0},{5,1},{6,2},{7,3},{8,4},{9,5},{1... | collective-permute-start | bytes 786440 | tf_op jit(solution)/shard_map/ppermute | solution.py:28
  81.5 20.4 %collective-permute-start.10 = (bf16[128,3072]{1,0:T(8,128)(2,1)S(1)}, bf16[128,3072]{1,0:T(8,128)(2,1)S(1)}, u32[]{:S(2)}, u32[]{:S(2)}) collective-permute-start(bf16[128,3072]{1,0:T(8,128)(2,1)S(1)} %pad_maximum_fusion.2), channel_id=1, source_target_pairs={{0,1},{1,0},{2,3},{3,2},{4,5},{5,4},{6,7},{7,6},{8,9},{9,8},{10,11... | collective-permute-start | bytes 2359304 | tf_op jit(solution)/shard_map/ppermute | solution.py:28
  98.4 12.9 %collective-permute-start.14 = (bf16[128,1024]{1,0:T(8,128)(2,1)S(1)}, bf16[128,1024]{1,0:T(8,128)(2,1)S(1)}, u32[]{:S(2)}, u32[]{:S(2)}) collective-permute-start(bf16[128,1024]{1,0:T(8,128)(2,1)S(1)} %collective-permute-done.12.a0.held), channel_id=1, source_target_pairs={{0,12},{1,13},{2,14},{3,15},{4,0},{5,1},{6,2},{7,3},{8,4},{9,5},{1... | collective-permute-start | bytes 786440 | tf_op jit(solution)/shard_map/ppermute | solution.py:28
  100.6 12.2 %collective-permute-start.15 = (bf16[128,1024]{1,0:T(8,128)(2,1)S(1)}, bf16[128,1024]{1,0:T(8,128)(2,1)S(1)}, u32[]{:S(2)}, u32[]{:S(2)}) collective-permute-start(bf16[128,1024]{1,0:T(8,128)(2,1)S(1)} %collective-permute-done.12.a0.held), channel_id=1, source_target_pairs={{0,8},{1,9},{2,10},{3,11},{4,12},{5,13},{6,14},{7,15},{8,0},{9,1},... | collective-permute-start | bytes 786440 | tf_op jit(solution)/shard_map/ppermute | solution.py:28
  114.9 19.1 %collective-permute-start.17 = (bf16[128,3072]{1,0:T(8,128)(2,1)S(1)}, bf16[128,3072]{1,0:T(8,128)(2,1)S(1)}, u32[]{:S(2)}, u32[]{:S(2)}) collective-permute-start(bf16[128,3072]{1,0:T(8,128)(2,1)S(1)} %pad_maximum_fusion.3), channel_id=1, source_target_pairs={{0,1},{1,0},{2,3},{3,2},{4,5},{5,4},{6,7},{7,6},{8,9},{9,8},{10,11... | collective-permute-start | bytes 2359304 | tf_op jit(solution)/shard_map/ppermute | solution.py:28
  132.2 12.3 %collective-permute-start.21 = (bf16[128,1024]{1,0:T(8,128)(2,1)S(1)}, bf16[128,1024]{1,0:T(8,128)(2,1)S(1)}, u32[]{:S(2)}, u32[]{:S(2)}) collective-permute-start(bf16[128,1024]{1,0:T(8,128)(2,1)S(1)} %collective-permute-done.19.a0.c), channel_id=1, source_target_pairs={{0,12},{1,13},{2,14},{3,15},{4,0},{5,1},{6,2},{7,3},{8,4},{9,5},{1... | collective-permute-start | bytes 786440 | tf_op jit(solution)/shard_map/ppermute | solution.py:28
  146.7 20.3 %collective-permute-start.24 = (bf16[128,3072]{1,0:T(8,128)(2,1)S(1)}, bf16[128,3072]{1,0:T(8,128)(2,1)S(1)}, u32[]{:S(2)}, u32[]{:S(2)}) collective-permute-start(bf16[128,3072]{1,0:T(8,128)(2,1)S(1)} %pad_maximum_fusion.4), channel_id=1, source_target_pairs={{0,1},{1,0},{2,3},{3,2},{4,5},{5,4},{6,7},{7,6},{8,9},{9,8},{10,11... | collective-permute-start | bytes 2359304 | tf_op jit(solution)/shard_map/ppermute | solution.py:28
  150.9 12.0 %collective-permute-start.26 = (bf16[128,1024]{1,0:T(8,128)(2,1)S(1)}, bf16[128,1024]{1,0:T(8,128)(2,1)S(1)}, u32[]{:S(2)}, u32[]{:S(2)}) collective-permute-start(bf16[128,1024]{1,0:T(8,128)(2,1)S(1)} %get-tuple-element.69.result), channel_id=1, source_target_pairs={{0,16},{1,18},{2,17},{3,19},{4,20},{5,22},{6,21},{7,23},{8,24},{9,... | collective-permute-start | bytes 786440 | tf_op jit(solution)/shard_map/ppermute | solution.py:28
  164.0 12.4 %collective-permute-start.28 = (bf16[128,1024]{1,0:T(8,128)(2,1)S(1)}, bf16[128,1024]{1,0:T(8,128)(2,1)S(1)}, u32[]{:S(2)}, u32[]{:S(2)}) collective-permute-start(bf16[128,1024]{1,0:T(8,128)(2,1)S(1)} %collective-permute-done.26.a0.c), channel_id=1, source_target_pairs={{0,12},{1,13},{2,14},{3,15},{4,0},{5,1},{6,2},{7,3},{8,4},{9,5},{1... | collective-permute-start | bytes 786440 | tf_op jit(solution)/shard_map/ppermute | solution.py:28
  165.8 12.1 %collective-permute-start.29 = (bf16[128,1024]{1,0:T(8,128)(2,1)S(1)}, bf16[128,1024]{1,0:T(8,128)(2,1)S(1)}, u32[]{:S(2)}, u32[]{:S(2)}) collective-permute-start(bf16[128,1024]{1,0:T(8,128)(2,1)S(1)} %collective-permute-done.26.a0.c), channel_id=1, source_target_pairs={{0,8},{1,9},{2,10},{3,11},{4,12},{5,13},{6,14},{7,15},{8,0},{9,1},... | collective-permute-start | bytes 786440 | tf_op jit(solution)/shard_map/ppermute | solution.py:28
  180.0 19.5 %collective-permute-start.31 = (bf16[128,3072]{1,0:T(8,128)(2,1)S(1)}, bf16[128,3072]{1,0:T(8,128)(2,1)S(1)}, u32[]{:S(2)}, u32[]{:S(2)}) collective-permute-start(bf16[128,3072]{1,0:T(8,128)(2,1)S(1)} %pad_maximum_fusion.5), channel_id=1, source_target_pairs={{0,1},{1,0},{2,3},{3,2},{4,5},{5,4},{6,7},{7,6},{8,9},{9,8},{10,11... | collective-permute-start | bytes 2359304 | tf_op jit(solution)/shard_map/ppermute | solution.py:28
  184.1 12.4 %collective-permute-start.33 = (bf16[128,1024]{1,0:T(8,128)(2,1)S(1)}, bf16[128,1024]{1,0:T(8,128)(2,1)S(1)}, u32[]{:S(2)}, u32[]{:S(2)}) collective-permute-start(bf16[128,1024]{1,0:T(8,128)(2,1)S(1)} %get-tuple-element.73.result), channel_id=1, source_target_pairs={{0,16},{1,18},{2,17},{3,19},{4,20},{5,22},{6,21},{7,23},{8,24},{9,... | collective-permute-start | bytes 786440 | tf_op jit(solution)/shard_map/ppermute | solution.py:28
  197.7 12.3 %collective-permute-start.35 = (bf16[128,1024]{1,0:T(8,128)(2,1)S(1)}, bf16[128,1024]{1,0:T(8,128)(2,1)S(1)}, u32[]{:S(2)}, u32[]{:S(2)}) collective-permute-start(bf16[128,1024]{1,0:T(8,128)(2,1)S(1)} %collective-permute-done.33.a0.c), channel_id=1, source_target_pairs={{0,12},{1,13},{2,14},{3,15},{4,0},{5,1},{6,2},{7,3},{8,4},{9,5},{1... | collective-permute-start | bytes 786440 | tf_op jit(solution)/shard_map/ppermute | solution.py:28
  212.2 20.3 %collective-permute-start.38 = (bf16[128,3072]{1,0:T(8,128)(2,1)S(1)}, bf16[128,3072]{1,0:T(8,128)(2,1)S(1)}, u32[]{:S(2)}, u32[]{:S(2)}) collective-permute-start(bf16[128,3072]{1,0:T(8,128)(2,1)S(1)} %pad_maximum_fusion.6), channel_id=1, source_target_pairs={{0,1},{1,0},{2,3},{3,2},{4,5},{5,4},{6,7},{7,6},{8,9},{9,8},{10,11... | collective-permute-start | bytes 2359304 | tf_op jit(solution)/shard_map/ppermute | solution.py:28
  229.5 12.3 %collective-permute-start.42 = (bf16[128,1024]{1,0:T(8,128)(2,1)S(1)}, bf16[128,1024]{1,0:T(8,128)(2,1)S(1)}, u32[]{:S(2)}, u32[]{:S(2)}) collective-permute-start(bf16[128,1024]{1,0:T(8,128)(2,1)S(1)} %collective-permute-done.40.a0.c), channel_id=1, source_target_pairs={{0,12},{1,13},{2,14},{3,15},{4,0},{5,1},{6,2},{7,3},{8,4},{9,5},{1... | collective-permute-start | bytes 786440 | tf_op jit(solution)/shard_map/ppermute | solution.py:28
  231.3 12.1 %collective-permute-start.43 = (bf16[128,1024]{1,0:T(8,128)(2,1)S(1)}, bf16[128,1024]{1,0:T(8,128)(2,1)S(1)}, u32[]{:S(2)}, u32[]{:S(2)}) collective-permute-start(bf16[128,1024]{1,0:T(8,128)(2,1)S(1)} %collective-permute-done.40.a0.c), channel_id=1, source_target_pairs={{0,8},{1,9},{2,10},{3,11},{4,12},{5,13},{6,14},{7,15},{8,0},{9,1},... | collective-permute-start | bytes 786440 | tf_op jit(solution)/shard_map/ppermute | solution.py:28
  245.5 19.1 %collective-permute-start.45 = (bf16[128,3072]{1,0:T(8,128)(2,1)S(1)}, bf16[128,3072]{1,0:T(8,128)(2,1)S(1)}, u32[]{:S(2)}, u32[]{:S(2)}) collective-permute-start(bf16[128,3072]{1,0:T(8,128)(2,1)S(1)} %pad_maximum_fusion.7), channel_id=1, source_target_pairs={{0,1},{1,0},{2,3},{3,2},{4,5},{5,4},{6,7},{7,6},{8,9},{9,8},{10,11... | collective-permute-start | bytes 2359304 | tf_op jit(solution)/shard_map/ppermute | solution.py:28
  262.8 12.3 %collective-permute-start.49 = (bf16[128,1024]{1,0:T(8,128)(2,1)S(1)}, bf16[128,1024]{1,0:T(8,128)(2,1)S(1)}, u32[]{:S(2)}, u32[]{:S(2)}) collective-permute-start(bf16[128,1024]{1,0:T(8,128)(2,1)S(1)} %collective-permute-done.47.a0.c), channel_id=1, source_target_pairs={{0,12},{1,13},{2,14},{3,15},{4,0},{5,1},{6,2},{7,3},{8,4},{9,5},{1... | collective-permute-start | bytes 786440 | tf_op jit(solution)/shard_map/ppermute | solution.py:28
  277.3 20.3 %collective-permute-start.52 = (bf16[128,3072]{1,0:T(8,128)(2,1)S(1)}, bf16[128,3072]{1,0:T(8,128)(2,1)S(1)}, u32[]{:S(2)}, u32[]{:S(2)}) collective-permute-start(bf16[128,3072]{1,0:T(8,128)(2,1)S(1)} %pad_maximum_fusion.8), channel_id=1, source_target_pairs={{0,1},{1,0},{2,3},{3,2},{4,5},{5,4},{6,7},{7,6},{8,9},{9,8},{10,11... | collective-permute-start | bytes 2359304 | tf_op jit(solution)/shard_map/ppermute | solution.py:28
  294.6 12.3 %collective-permute-start.56 = (bf16[128,1024]{1,0:T(8,128)(2,1)S(1)}, bf16[128,1024]{1,0:T(8,128)(2,1)S(1)}, u32[]{:S(2)}, u32[]{:S(2)}) collective-permute-start(bf16[128,1024]{1,0:T(8,128)(2,1)S(1)} %collective-permute-done.54.a0.c), channel_id=1, source_target_pairs={{0,12},{1,13},{2,14},{3,15},{4,0},{5,1},{6,2},{7,3},{8,4},{9,5},{1... | collective-permute-start | bytes 786440 | tf_op jit(solution)/shard_map/ppermute | solution.py:28
  296.4 12.1 %collective-permute-start.57 = (bf16[128,1024]{1,0:T(8,128)(2,1)S(1)}, bf16[128,1024]{1,0:T(8,128)(2,1)S(1)}, u32[]{:S(2)}, u32[]{:S(2)}) collective-permute-start(bf16[128,1024]{1,0:T(8,128)(2,1)S(1)} %collective-permute-done.54.a0.c), channel_id=1, source_target_pairs={{0,8},{1,9},{2,10},{3,11},{4,12},{5,13},{6,14},{7,15},{8,0},{9,1},... | collective-permute-start | bytes 786440 | tf_op jit(solution)/shard_map/ppermute | solution.py:28
  311.4 19.2 %collective-permute-start.59 = (bf16[128,3072]{1,0:T(8,128)(2,1)}, bf16[128,3072]{1,0:T(8,128)(2,1)S(1)}, u32[]{:S(2)}, u32[]{:S(2)}) collective-permute-start(bf16[128,3072]{1,0:T(8,128)(2,1)} %pad_maximum_fusion.9), channel_id=1, source_target_pairs={{0,1},{1,0},{2,3},{3,2},{4,5},{5,4},{6,7},{7,6},{8,9},{9,8},{10,11... | collective-permute-start | bytes 2359304 | tf_op jit(solution)/shard_map/ppermute | solution.py:28
  327.9 12.3 %collective-permute-start.63 = (bf16[128,1024]{1,0:T(8,128)(2,1)S(1)}, bf16[128,1024]{1,0:T(8,128)(2,1)S(1)}, u32[]{:S(2)}, u32[]{:S(2)}) collective-permute-start(bf16[128,1024]{1,0:T(8,128)(2,1)S(1)} %collective-permute-done.61.a0.c), channel_id=1, source_target_pairs={{0,12},{1,13},{2,14},{3,15},{4,0},{5,1},{6,2},{7,3},{8,4},{9,5},{1... | collective-permute-start | bytes 786440 | tf_op jit(solution)/shard_map/ppermute | solution.py:28
  347.5 18.6 %collective-permute-start.66 = (bf16[128,3072]{1,0:T(8,128)(2,1)S(1)}, bf16[128,3072]{1,0:T(8,128)(2,1)S(1)}, u32[]{:S(2)}, u32[]{:S(2)}) collective-permute-start(bf16[128,3072]{1,0:T(8,128)(2,1)S(1)} %pad_maximum_fusion.10), channel_id=1, source_target_pairs={{0,1},{1,0},{2,3},{3,2},{4,5},{5,4},{6,7},{7,6},{8,9},{9,8},{10,11... | collective-permute-start | bytes 2359304 | tf_op jit(solution)/shard_map/ppermute | solution.py:28
  363.0 12.3 %collective-permute-start.70 = (bf16[128,1024]{1,0:T(8,128)(2,1)S(1)}, bf16[128,1024]{1,0:T(8,128)(2,1)S(1)}, u32[]{:S(2)}, u32[]{:S(2)}) collective-permute-start(bf16[128,1024]{1,0:T(8,128)(2,1)S(1)} %collective-permute-done.68.a0.c), channel_id=1, source_target_pairs={{0,12},{1,13},{2,14},{3,15},{4,0},{5,1},{6,2},{7,3},{8,4},{9,5},{1... | collective-permute-start | bytes 786440 | tf_op jit(solution)/shard_map/ppermute | solution.py:28
  364.8 12.1 %collective-permute-start.71 = (bf16[128,1024]{1,0:T(8,128)(2,1)S(1)}, bf16[128,1024]{1,0:T(8,128)(2,1)S(1)}, u32[]{:S(2)}, u32[]{:S(2)}) collective-permute-start(bf16[128,1024]{1,0:T(8,128)(2,1)S(1)} %collective-permute-done.68.a0.c), channel_id=1, source_target_pairs={{0,8},{1,9},{2,10},{3,11},{4,12},{5,13},{6,14},{7,15},{8,0},{9,1},... | collective-permute-start | bytes 786440 | tf_op jit(solution)/shard_map/ppermute | solution.py:28
  388.7 17.5 %all-to-all-start.1 = ((bf16[16,4,8,512]{3,2,1,0:T(8,128)(2,1)}), bf16[16,4,8,512]{3,2,1,0:T(8,128)(2,1)S(1)}, u32[]{:S(2)}, u32[]{:S(2)}) async-start(bf16[16,4,8,512]{3,2,1,0:T(8,128)(2,1)} %copy.11), calls=%async_computation.1 | async-start | bytes 1048576 | tf_op jit(solution)/shard_map/all_to_all | solution.py:346
  (70 other events, 396.6 us)
